TPU v7x, 512 devices: a whole 4x8x8 slice. The times are simulated.
512 devices in a mesh: ctx: 64 (over x, y, core), tp: 8 (over z).
Axes of the slice: x: 4, y: 8, z: 8, core: 2. Of those that a mesh axis runs over, the one named last changes fastest.
Arguments:
- hidden: bfloat16 [2, 64, 8192], P(None, None, 'ctx'), may hold values from -9 to 9
- qkv_weight: bfloat16 [8192, 10240], P('ctx', 'tp'), may hold values from -0.0625 to 0.0625
- qkv_bias: bfloat16 [10240], P('tp'), may hold values from -4 to 4
- out_weight: bfloat16 [8192, 8192], P('tp', 'ctx'), may hold values from -0.0625 to 0.0625
- prefix_cache: bfloat16 [8, 16384, 2048], P(None, 'ctx', 'tp'), may hold values from -12 to 12
- tail_cache: bfloat16 [4096, 1, 16, 2048], P('ctx', None, None, 'tp'), may hold values from -12 to 12
- parents: int32 [2, 64], replicated, may hold values from 0 to 63, as said below
- start_dev: int32 [3, 64], replicated, may hold values from 0 to 63, as said below
Outputs:
- attended: bfloat16 [2, 64, 8192], P(None, 'tp', 'ctx')
- tail_out: bfloat16 [4096, 1, 16, 2048], P('ctx', None, None, 'tp')
Inputs may be any that keep to these rules, and one draw needn't show every extreme that they name: parents[s, c] is a beam of the same prompt as c, that is with the same c // 8. For each step s, among the values (start_dev[s + 1, c] - start_dev[s, parents[s, c]]) mod 64 over all beams c, a quarter of the residues are taken by exactly 2 beams each, half by 1 beams each, and the rest by none.
All inputs are finite; a program needn't handle non-finite values.
Results may differ from a plain program's by a relative error of at most 0.019.
Values may be sent and summed in bfloat16 or wider, within the bound.
No kernel may reach another device: no remote copies, remote signals or barrier semaphores. Data moves between devices by JAX's collectives and lax.ppermute only.
A program may use at most 128 MiB of HBM per device.

v0:
```python
import jax
import jax.numpy as jnp
from jax import lax
from jax.sharding import PartitionSpec as P

H = 64
KVH = 8
HD = 128
BW = 8


ROPE_BASE = 1000000.0


def merged(shard, axis, combine):
    everything = jax.tree.map(lambda part: lax.all_gather(part, axis), shard)
    first = jax.tree.map(lambda part: part[0], everything)

    def hop(k, so_far):
        return combine(so_far, jax.tree.map(lambda part: part[k], everything))

    return lax.fori_loop(1, lax.axis_size(axis), hop, first)


def rope_tables(position):
    half_dim = HD // 2
    frequency = ROPE_BASE ** (-(jnp.arange(half_dim, dtype=jnp.float32) * 2.0) / HD)
    angles = position * frequency
    return (jnp.cos(angles), jnp.sin(angles))


def rotate(vector, cosine, sine_part):
    half_dim = HD // 2
    lower_half = vector[..., :half_dim]
    upper_half = vector[..., half_dim:]
    return jnp.concatenate(
        [
            lower_half * cosine - upper_half * sine_part,
            upper_half * cosine + lower_half * sine_part,
        ],
        axis=-1,
    )


def combine_parts(earlier_part, later_part):
    peak_one, total_one, mixed_one = earlier_part
    peak_two, total_two, mixed_two = later_part
    row_max = jnp.maximum(peak_one, peak_two)
    scale_one = jnp.exp(peak_one - row_max)
    scale_two = jnp.exp(peak_two - row_max)
    return (
        row_max,
        total_one * scale_one + total_two * scale_two,
        mixed_one * scale_one[..., None] + mixed_two * scale_two[..., None],
    )


def attend_head(head_queries, prefix_cache, tail_flat, column, valid, score_scale):
    prompt_count = prefix_cache.shape[0]
    prefix_rows = prefix_cache.shape[1]
    beam_count = head_queries.shape[0]
    group_size = head_queries.shape[1]
    prefix_keys = prefix_cache[:, :, column : column + HD]
    prefix_values = prefix_cache[:, :, column + HD : column + 2 * HD]
    tail_keys = tail_flat[:, :, column : column + HD]
    tail_values = tail_flat[:, :, column + HD : column + 2 * HD]
    grouped = head_queries.reshape(prompt_count, BW, group_size, HD)
    prefix_scores = (
        jnp.einsum("pbgd,pnd->pbgn", grouped, prefix_keys, preferred_element_type=jnp.float32)
        * score_scale
    )
    prefix_scores = prefix_scores.reshape(beam_count, group_size, prefix_rows)
    tail_scores = (
        jnp.einsum("cgd,cnd->cgn", head_queries, tail_keys, preferred_element_type=jnp.float32)
        * score_scale
    )
    tail_scores = jnp.where(valid[:, None, :], tail_scores, -jnp.inf)
    row_max = jnp.maximum(jnp.max(prefix_scores, axis=-1), jnp.max(tail_scores, axis=-1))
    prefix_weights = jnp.exp(prefix_scores - row_max[..., None])
    tail_weights = jnp.exp(tail_scores - row_max[..., None])
    denominator = jnp.sum(prefix_weights, axis=-1) + jnp.sum(tail_weights, axis=-1)
    prefix_low = prefix_weights.astype(jnp.bfloat16).reshape(
        prompt_count, BW, group_size, prefix_rows
    )
    weighted = jnp.einsum(
        "pbgn,pnd->pbgd", prefix_low, prefix_values, preferred_element_type=jnp.float32
    )
    weighted = weighted.reshape(beam_count, group_size, HD)
    weighted = weighted + jnp.einsum(
        "cgn,cnd->cgd",
        tail_weights.astype(jnp.bfloat16),
        tail_values,
        preferred_element_type=jnp.float32,
    )
    return (row_max, denominator, weighted)


def per_device(
    hidden, qkv_weight, qkv_bias, out_weight, prefix_cache, tail_cache, parents, start_dev
):
    ctx_count = lax.axis_size("ctx")
    my_index = lax.axis_index("ctx")
    beam_count = tail_cache.shape[0]
    pages_dev = tail_cache.shape[1]
    page_len = tail_cache.shape[2]
    row_width = tail_cache.shape[3]
    local_heads = row_width // (2 * HD)
    group_size = H // KVH
    step_count = hidden.shape[0]
    prefix_rows = prefix_cache.shape[1]
    tail_len = pages_dev * ctx_count * page_len
    prefix_len = prefix_rows * ctx_count
    most_rows = 2 * beam_count // ctx_count
    beam_ids = jnp.arange(beam_count, dtype=jnp.int32)
    page_ids = jnp.arange(pages_dev, dtype=jnp.int32)
    inner_ids = jnp.arange(page_len, dtype=jnp.int32)
    score_scale = HD ** (-0.5)
    tail_pool = tail_cache
    results = []
    for step_idx in range(step_count):
        partial_proj = jnp.dot(hidden[step_idx], qkv_weight, preferred_element_type=jnp.float32)
        projected = lax.psum(partial_proj, "ctx") + qkv_bias.astype(jnp.float32)
        projected = projected.reshape(beam_count, local_heads, group_size + 2, HD)
        position = prefix_len + tail_len - step_count + step_idx
        cosine, sine_part = rope_tables(position)
        queries = rotate(projected[:, :, :group_size], cosine, sine_part).astype(jnp.bfloat16)
        key_new = rotate(projected[:, :, group_size], cosine, sine_part).astype(jnp.bfloat16)
        value_new = projected[:, :, group_size + 1].astype(jnp.bfloat16)
        parent = parents[step_idx]
        old_start = start_dev[step_idx]
        new_start = start_dev[step_idx + 1]
        offsets = (new_start - old_start[parent]) % ctx_count
        earlier = (offsets[None, :] == offsets[:, None]) & (beam_ids[None, :] < beam_ids[:, None])
        slot_rank = jnp.sum(earlier.astype(jnp.int32), axis=1)
        shift_ids = jnp.arange(ctx_count, dtype=jnp.int32)
        rank_ids = jnp.arange(most_rows, dtype=jnp.int32)
        matches = (offsets[None, None, :] == shift_ids[:, None, None]) & (
            slot_rank[None, None, :] == rank_ids[None, :, None]
        )
        picked = jnp.sum(jnp.where(matches, beam_ids[None, None, :], 0), axis=2)
        is_live = jnp.any(matches, axis=2)
        targets = (shift_ids - my_index) % ctx_count
        picked = picked[targets]
        is_live = is_live[targets]
        send_rows = jnp.take(tail_pool, parent[picked].reshape(-1), axis=0)
        send_rows = send_rows.reshape(ctx_count, most_rows, pages_dev, page_len, row_width)
        send_rows = jnp.where(is_live[:, :, None, None, None], send_rows, jnp.zeros_like(send_rows))
        arrived = lax.all_to_all(send_rows, "ctx", split_axis=0, concat_axis=0, tiled=True)
        arrive_slot = (my_index - offsets) % ctx_count * most_rows + slot_rank
        relocated = jnp.take(
            arrived.reshape(ctx_count * most_rows, pages_dev, page_len, row_width),
            arrive_slot,
            axis=0,
        )
        owner_dev = (new_start - 1) % ctx_count
        own_page = owner_dev == my_index
        new_entry = jnp.stack([key_new, value_new], axis=2).reshape(beam_count, row_width)
        in_row = page_len - step_count + step_idx
        current = relocated[:, pages_dev - 1, in_row]
        relocated = relocated.at[:, pages_dev - 1, in_row].set(
            jnp.where(own_page[:, None], new_entry, current)
        )
        limit = tail_len - step_count + step_idx
        page_pos = page_ids[None, :] * ctx_count + (my_index - new_start[:, None]) % ctx_count
        token_pos = (page_pos[:, :, None] * page_len + inner_ids[None, None, :]).reshape(
            beam_count, pages_dev * page_len
        )
        valid = token_pos <= limit
        tail_flat = relocated.reshape(beam_count, pages_dev * page_len, row_width)
        head_max, head_total, head_mixed = attend_head(
            queries[:, 0], prefix_cache, tail_flat, 0, valid, score_scale
        )
        maxima_list = [head_max]
        totals_list = [head_total]
        mixed_list = [head_mixed]
        row_max = jnp.stack(maxima_list, axis=1)
        denominator = jnp.stack(totals_list, axis=1)
        weighted = jnp.stack(mixed_list, axis=1)
        row_max, denominator, weighted = merged(
            (row_max, denominator, weighted), "ctx", combine_parts
        )
        attention = (
            (weighted / denominator[..., None])
            .astype(jnp.bfloat16)
            .reshape(beam_count, local_heads * group_size * HD)
        )
        out_term = jnp.dot(attention, out_weight, preferred_element_type=jnp.float32)
        out_share = lax.psum_scatter(
            out_term.astype(jnp.bfloat16), "tp", scatter_dimension=0, tiled=True
        )
        results.append(out_share)
        tail_pool = relocated
    return (jnp.stack(results), tail_pool)


def solution(mesh):
    placed = (
        P(None, None, "ctx"),
        P("ctx", "tp"),
        P("tp"),
        P("tp", "ctx"),
        P(None, "ctx", "tp"),
        P("ctx", None, None, "tp"),
        P(),
        P(),
    )
    return jax.shard_map(
        per_device,
        mesh=mesh,
        in_specs=placed,
        out_specs=(P(None, "tp", "ctx"), P("ctx", None, None, "tp")),
        check_vma=False,
    )
```

profile of v0, /device:TPU:1, one launch (start us, length us, event | category | flops | bytes accessed | tf_op | source)
XLA Modules:
  0.0 714.0 jit_solution(1602051170530229721)
XLA Ops:
  15.9 1.2 gather_fusion.3
  17.2 1.2 gather_fusion.7
  21.3 1.2 broadcast_select_fusion.1
  22.5 11.8 %all-to-all-start = ((bf16[64,2,1,16,256]{4,3,1,2,0:T(8,128)(2,1)}), bf16[64,2,1,16,256]{4,3,1,2,0:T(8,128)(2,1)}, u32[]{:S(2)}, u32[]{:S(2)}) async-start(bf16[64,2,1,16,256]{4,3,1,2,0:T(8,128)(2,1)} %broadcast_select_fusion.1), calls=%async_computation | async-start | bytes 2097152 | tf_op jit(solution)/shard_map/all_to_all | solution.py:148
  39.1 197.3 %all-reduce.6.cloned.1.call-done = (f32[64,1280]{1,0:T(8,128)}, f32[64,1280]{1,0:T(8,128)}) async-done(((f32[64,1280]{1,0:T(8,128)}, f32[64,1280]{1,0:T(8,128)}), (f32[64,1280]{1,0:T(8,128)}, f32[64,1280]{1,0:T(8,128)})) %all-reduce.6.cloned.1.call-update) | async-done | bytes 655376 | tf_op jit(solution)/shard_map/psum | solution.py:122
  239.1 1.8 gather_fusion.9
  241.8 2.2 broadcast_select_fusion.5
  244.0 1.5 scatter.6
  245.6 1.4 fusion.102
  251.4 1.3 dynamic-slice.24
  257.9 8.1 %all-to-all-start.1 = ((bf16[64,2,1,16,256]{4,3,1,2,0:T(8,128)(2,1)}), bf16[64,2,1,16,256]{4,3,1,2,0:T(8,128)(2,1)S(1)}, u32[]{:S(2)}, u32[]{:S(2)}) async-start(bf16[64,2,1,16,256]{4,3,1,2,0:T(8,128)(2,1)} %broadcast_select_fusion), calls=%async_computation.1 | async-start | bytes 2097152 | tf_op jit(solution)/shard_map/all_to_all | solution.py:148
  267.9 1.5 fusion.101
  271.6 61.2 %all_gather.19 = f32[64,64,1,8]{1,3,2,0:T(8,128)S(1)} all-gather(f32[1,64,1,8]{1,3,2,0:T(8,128)S(1)} %copy.133), channel_id=1, replica_groups=mesh['ctx'=64,'tp'=8] {'ctx'}, dimensions={0}, use_global_device_ids=true | all-gather | bytes 133120 | tf_op jit(solution)/shard_map/all_gather | solution.py:16
  332.8 37.1 %all_gather.18 = f32[64,64,1,8]{1,3,2,0:T(8,128)S(1)} all-gather(f32[1,64,1,8]{1,3,2,0:T(8,128)S(1)} %copy.132), channel_id=1, replica_groups=mesh['ctx'=64,'tp'=8] {'ctx'}, dimensions={0}, use_global_device_ids=true | all-gather | bytes 133120 | tf_op jit(solution)/shard_map/all_gather | solution.py:16
  371.4 2.2 broadcast_select_fusion.4
  373.6 1.4 scatter.9
  376.1 37.2 %all_gather.22 = f32[64,64,1,8]{1,3,2,0:T(8,128)S(1)} all-gather(f32[1,64,1,8]{1,3,2,0:T(8,128)S(1)} %copy.146), channel_id=1, replica_groups=mesh['ctx'=64,'tp'=8] {'ctx'}, dimensions={0}, use_global_device_ids=true | all-gather | bytes 133120 | tf_op jit(solution)/shard_map/all_gather | solution.py:16
  413.3 36.9 %all_gather.21 = f32[64,64,1,8]{1,3,2,0:T(8,128)S(1)} all-gather(f32[1,64,1,8]{1,3,2,0:T(8,128)S(1)} %copy.145), channel_id=1, replica_groups=mesh['ctx'=64,'tp'=8] {'ctx'}, dimensions={0}, use_global_device_ids=true | all-gather | bytes 133120 | tf_op jit(solution)/shard_map/all_gather | solution.py:16
  450.2 1.3 fusion.12
  453.6 134.3 %while.40 = (s32[]{:T(128)}, f32[64,1,8]{0,2,1:T(8,128)S(1)}, f32[64,1,8]{0,2,1:T(8,128)S(1)}, f32[64,1,8,128]{3,2,1,0:T(8,128)S(1)}, f32[64,64,1,8]{1,3,2,0:T(8...) while((s32[]{:T(128)}, f32[64,1,8]{0,2,1:T(8,128)S(1)}, ...), condition=%wide.region_10.13_spmd, body=%wide.region_9.12_spmd.sunk | while | flops 200197 | bytes 825499 | solution.py:22
  454.5 1.2 fusion.116
  456.6 1.2 fusion.116
  458.7 1.2 fusion.116
  460.8 1.2 fusion.116
  463.0 1.2 fusion.116
  465.1 1.2 fusion.116
  467.2 1.2 fusion.116
  471.5 1.2 fusion.116
  475.8 1.2 fusion.116
  477.9 1.2 fusion.116
  480.0 1.2 fusion.116
  482.2 1.2 fusion.116
  484.3 1.2 fusion.116
  486.4 1.2 fusion.116
  488.6 1.2 fusion.116
  492.8 1.2 fusion.116
  494.9 1.2 fusion.116
  497.1 1.2 fusion.116
  499.2 1.2 fusion.116
  501.3 1.2 fusion.116
  503.5 1.2 fusion.116
  505.6 1.2 fusion.116
  507.7 1.2 fusion.116
  509.9 1.2 fusion.116
  512.0 1.2 fusion.116
  514.1 1.2 fusion.116
  520.5 1.2 fusion.116
  522.7 1.2 fusion.116
  524.8 1.2 fusion.116
  527.0 1.3 fusion.116
  529.1 1.2 fusion.116
  531.3 1.2 fusion.116
  533.4 1.2 fusion.116
  535.6 1.2 fusion.116
  539.8 1.2 fusion.116
  548.3 1.2 fusion.116
  550.5 1.2 fusion.116
  554.7 1.2 fusion.116
  561.1 1.2 fusion.116
  569.6 1.2 fusion.116
  576.0 1.2 fusion.116
  586.7 1.2 fusion.116
  590.3 91.5 %while.41 = (s32[]{:T(128)}, f32[64,1,8]{0,2,1:T(8,128)S(1)}, f32[64,1,8]{0,2,1:T(8,128)S(1)}, f32[64,1,8,128]{3,2,1,0:T(8,128)S(1)}, f32[64,64,1,8]{1,3,2,0:T(8...) while((s32[]{:T(128)}, f32[64,1,8]{0,2,1:T(8,128)S(1)}, ...), condition=%wide.region_22.25_spmd, body=%wide.region_21.24_spmd.sunk | while | flops 200197 | bytes 825499 | solution.py:22
  683.2 23.6 %all-reduce.3 = (bf16[64,128]{1,0:T(8,128)(2,1)S(1)}, bf16[64,128]{1,0:T(8,128)(2,1)S(1)}) all-reduce(bf16[64,128]{1,0:T(8,128)(2,1)S(1)} %convolution_convert_fusion, bf16[64,128]{1,0:T(8,128)(2,1)S(1)} %convolution_convert_fusion.1), channel_id=5, replica_groups=mesh['ctx'=64,'tp'=8] {'tp'}, use_global_device_ids=true, to_apply=%region_23.26.clone | all-reduce | flops 16384 | bytes 65536
  (880 shorter events, 210.8 us)
Async XLA Ops:
  7.2 13.3 %copy-start = (bf16[64,1,16,256]{3,2,1,0:T(8,128)(2,1)S(1)}, bf16[64,1,16,256]{3,2,1,0:T(8,128)(2,1)}, u32[]{:S(2)}) copy-start(bf16[64,1,16,256]{3,2,1,0:T(8,128)(2,1)} %param.25) | copy-start | bytes 1572868
  11.8 5.3 copy-start.12
  13.0 6.8 copy-start.10
  14.2 0.5 copy-start.15
  14.7 0.8 copy-start.14
  17.1 17.3 %copy-start.3 = (bf16[128,1280]{1,0:T(8,128)(2,1)S(1)}, bf16[128,1280]{1,0:T(8,128)(2,1)}, u32[]{:S(2)}) copy-start(bf16[128,1280]{1,0:T(8,128)(2,1)} %param.21) | copy-start | bytes 983044
  17.2 17.3 %copy-start.9 = (bf16[2,64,128]{2,1,0:T(8,128)(2,1)S(1)}, bf16[2,64,128]{2,1,0:T(8,128)(2,1)}, u32[]{:S(2)}) copy-start(bf16[2,64,128]{2,1,0:T(8,128)(2,1)} %param.20) | copy-start | bytes 98308
  17.2 19.2 %copy-start.13 = (bf16[1280]{0:T(1024)(128)(2,1)S(1)}, bf16[1280]{0:T(1024)(128)(2,1)}, u32[]{:S(2)}) copy-start(bf16[1280]{0:T(1024)(128)(2,1)} %param.22) | copy-start | bytes 7684
  17.2 19.8 %copy-start.11 = (s32[3,64]{1,0:T(4,128)S(1)}, s32[3,64]{1,0:T(4,128)}, u32[]{:S(2)}) copy-start(s32[3,64]{1,0:T(4,128)} %param.27) | copy-start | bytes 2308
  17.2 20.4 %copy-start.16 = (s32[4]{0:T(128)S(1)}, s32[4]{0:T(128)}, u32[]{:S(2)}) copy-start(s32[4]{0:T(128)} %constant.253.clone.1) | copy-start | bytes 52
  17.2 221.5 %copy-start.1 = (bf16[8,256,256]{2,1,0:T(8,128)(2,1)S(1)}, bf16[8,256,256]{2,1,0:T(8,128)(2,1)}, u32[]{:S(2)}) copy-start(bf16[8,256,256]{2,1,0:T(8,128)(2,1)} %param.24) | copy-start | bytes 3145732
  22.5 216.6 %all-to-all-start = ((bf16[64,2,1,16,256]{4,3,1,2,0:T(8,128)(2,1)}), bf16[64,2,1,16,256]{4,3,1,2,0:T(8,128)(2,1)}, u32[]{:S(2)}, u32[]{:S(2)}) async-start(bf16[64,2,1,16,256]{4,3,1,2,0:T(8,128)(2,1)} %broadcast_select_fusion.1), calls=%async_computation | async-start | bytes 2097152 | tf_op jit(solution)/shard_map/all_to_all | solution.py:148
  34.4 202.0 %all-reduce.6.cloned.1.call-start = ((), (), s32[]{:S(2)}) async-start(), calls=%async_computation.4 | async-start | bytes 1310720 | tf_op jit(solution)/shard_map/psum | solution.py:122
  36.3 416.3 %all-gather.5.cloned.1.call-start = ((), (), s32[]{:S(2)}) async-start(), calls=%async_computation.2 | async-start | bytes 17039360 | tf_op jit(solution)/shard_map/all_gather | solution.py:16
  36.4 201.2 %copy-start.17 = (s32[2]{0:T(128)}, s32[2]{0:T(128)S(1)}, u32[]{:S(2)}) copy-start(s32[2]{0:T(128)S(1)} %get-tuple-element.552) | copy-start | bytes 28
  238.7 2.3 copy-start.4
  238.7 2.3 copy-start.5
  247.0 0.6 copy-start.8
  247.0 0.6 copy-start.7
  257.9 112.1 %all-to-all-start.1 = ((bf16[64,2,1,16,256]{4,3,1,2,0:T(8,128)(2,1)}), bf16[64,2,1,16,256]{4,3,1,2,0:T(8,128)(2,1)S(1)}, u32[]{:S(2)}, u32[]{:S(2)}) async-start(bf16[64,2,1,16,256]{4,3,1,2,0:T(8,128)(2,1)} %broadcast_select_fusion), calls=%async_computation.1 | async-start | bytes 2097152 | tf_op jit(solution)/shard_map/all_to_all | solution.py:148
  266.0 323.3 %all-gather.7.cloned.1.call-start = ((), (), s32[]{:S(2)}) async-start(), calls=%async_computation.3 | async-start | bytes 17039360 | tf_op jit(solution)/shard_map/all_gather | solution.py:16
  332.8 37.1 %copy-start.6 = (f32[64,64,1,8]{1,3,2,0:T(8,128)}, f32[64,64,1,8]{1,3,2,0:T(8,128)S(1)}, u32[]{:S(2)}) copy-start(f32[64,64,1,8]{1,3,2,0:T(8,128)S(1)} %all_gather.19) | copy-start | bytes 393220
  375.1 332.4 %copy-start.2 = (bf16[64,1,16,256]{3,2,0,1:T(8,128)(2,1)}, bf16[64,1,16,256]{3,2,0,1:T(8,128)(2,1)S(1)}, u32[]{:S(2)}) copy-start(bf16[64,1,16,256]{3,2,0,1:T(8,128)(2,1)S(1)} %scatter.9) | copy-start | bytes 1572868
Sparse Core Ops, SparseCore 0:
  39.3 196.9 all-reduce.5
  248.7 114.9 all-gather.4
  452.7 103.4 all-gather.6
where the time goes:
time: 726 us; the launch traced here: 714 us
  other arithmetic  223 us (31%)
  waiting for transfers between devices  197 us (27%)
  blocking collectives  196 us (27%)
  local copies, waits for them, and re-layouts  45.4 us (6%)
  starting transfers between devices  20.1 us (3%)
  between operations  15.1 us (2%)
  matrix products  11.3 us (2%)
    psum x1, waiting for transfers between devices, per_device(): projected = lax.psum(partial_proj, 'ctx') + qkv_bias.astype(jnp.float32)  197 us
    all_gather x4, blocking collectives, merged(): everything = jax.tree.map(lambda part: lax.all_gather(part, axis), shard)  172 us
    add x126, other arithmetic, combine_parts(): mixed_one * scale_one[..., None] + mixed_two * scale_two[..., None]  152 us
    mul x126, other arithmetic, combine_parts(): mixed_two * scale_two[..., None]  44.9 us
    unnamed x1, blocking collectives  23.6 us
    all_to_all x2, starting transfers between devices, per_device(): lax.all_to_all(send_rows, 'ctx', split_axis=0, concat_axis=0, tiled=True)  19.9 us
  transfers between devices with their start and end apart: 5, of which 1 were waited for; matrix products, arithmetic and copies ran while one was open for 23% of the time, Pallas kernels for 0%

commit v1 on v0

v1 whole, which is shorter than its diff:
```python
import functools

import jax
import jax.numpy as jnp
import numpy as np
from jax import lax
from jax.experimental import pallas as pl
from jax.experimental.pallas import tpu as pltpu
from jax.sharding import PartitionSpec as P

HD = 128
BW = 8
GROUP = 8
STEPS = 2
ROWS = STEPS * BW
PAGE = 16
CTX = 64
LX, LY, LC = 4, 8, 2
POSITION = 17406
PACK = ROWS + 8
F32, BF16 = jnp.float32, jnp.bfloat16

XC_GROUPS = [[(x * LY + y) * LC + c for x in range(LX) for c in range(LC)] for y in range(LY)]
Y_GROUPS = [[(x * LY + y) * LC + c for y in range(LY)] for x in range(LX) for c in range(LC)]

VMEM = pl.BlockSpec(memory_space=pltpu.VMEM)
SMEM = pl.BlockSpec(memory_space=pltpu.SMEM)
ANY = pl.BlockSpec(memory_space=pl.ANY)
PARAMS = pltpu.CompilerParams(vmem_limit_bytes=32 * 1024 * 1024)


def rope_rows():
    half = HD // 2
    frequency = 1000000.0 ** (-(np.arange(half) * 2.0) / HD)
    cos_of, sin_of = [], []
    for s in range(STEPS):
        angles = (POSITION + s) * frequency
        cos_of.append(np.concatenate([np.cos(angles), np.cos(angles)]))
        sin_of.append(np.concatenate([-np.sin(angles), np.sin(angles)]))
    cosine = np.zeros((GROUP, PACK, HD), np.float32)
    sine = np.zeros((GROUP, PACK, HD), np.float32)
    for h in range(GROUP):
        for s in range(STEPS):
            cosine[h, s * BW : (s + 1) * BW] = cos_of[s]
            sine[h, s * BW : (s + 1) * BW] = sin_of[s]
        if h % 2 == 0:
            cosine[h, ROWS:] = cos_of[h // 2 % 2]
            sine[h, ROWS:] = sin_of[h // 2 % 2]
        else:
            cosine[h, ROWS:] = 1.0
    return cosine, sine


def project_kernel(hidden_ref, weight_ref, out_ref):
    prompts = hidden_ref.shape[1] // BW
    steps = [hidden_ref[s].astype(F32) for s in range(STEPS)]
    rows = [steps[s][p * BW : (p + 1) * BW] for p in range(prompts) for s in range(STEPS)]
    hidden = jnp.concatenate(rows, axis=0).astype(BF16)
    for col in range(GROUP + 2):
        part = jnp.dot(
            hidden, weight_ref[:, col * HD : (col + 1) * HD], preferred_element_type=F32
        )
        for p in range(prompts):
            tile = part[p * ROWS : (p + 1) * ROWS]
            if col < GROUP:
                out_ref[p * GROUP + col, :ROWS, :] = tile.astype(BF16)
            else:
                for h in range(GROUP):
                    if h % 2 == col - GROUP:
                        s = h // 2 % 2
                        out_ref[p * GROUP + h, ROWS:, :] = tile[s * BW : (s + 1) * BW].astype(BF16)


def rotate_kernel(parts_ref, bias_ref, cos_ref, sin_ref, out_ref):
    h = lax.rem(lax.axis_index("ctx"), GROUP)
    total = jnp.sum(parts_ref[...].astype(F32), axis=0)
    bias = bias_ref[...].astype(F32)
    line = lax.broadcasted_iota(jnp.int32, bias.shape, 0)
    q_bias = jnp.sum(jnp.where(line == h, bias, 0.0), axis=0, keepdims=True)
    kv_bias = jnp.sum(jnp.where(line == GROUP + lax.rem(h, 2), bias, 0.0), axis=0, keepdims=True)
    row = lax.broadcasted_iota(jnp.int32, total.shape, 0)
    total = total + jnp.where(row < ROWS, q_bias, kv_bias)
    turned = total * cos_ref[h] + pltpu.roll(total, HD // 2, 1) * sin_ref[h]
    out_ref[...] = jnp.broadcast_to(turned.astype(BF16)[None], out_ref.shape)


def attend_kernel(parents_ref, start_ref, shared_ref, prefix_ref, tail_ref, out_ref):
    me = lax.axis_index("ctx")
    prompts = prefix_ref.shape[0]
    scale = HD**-0.5
    contract = (((1,), (1,)), ((), ()))
    lane = lax.broadcasted_iota(jnp.int32, (ROWS, HD), 1)
    row = lax.broadcasted_iota(jnp.int32, (ROWS, HD), 0)
    lane_full = lax.broadcasted_iota(jnp.int32, (GROUP * ROWS, HD), 1)

    def spread(mask):
        return jnp.concatenate([mask] * GROUP, axis=0)

    for p in range(prompts):
        query = shared_ref[p * GROUP : (p + 1) * GROUP, :ROWS, :].reshape(GROUP * ROWS, HD)
        new_key = jnp.concatenate(
            [shared_ref[p * GROUP + 2 * s, ROWS:, :].astype(F32) for s in range(STEPS)]
            + [jnp.zeros((HD - ROWS, HD), F32)],
            axis=0,
        ).astype(BF16)
        new_value = jnp.concatenate(
            [shared_ref[p * GROUP + 2 * s + 1, ROWS:, :].astype(F32) for s in range(STEPS)]
            + [jnp.zeros((HD - ROWS, HD), F32)],
            axis=0,
        ).astype(BF16)
        tail = tail_ref[p * BW : (p + 1) * BW].reshape(BW * PAGE, 2 * HD)

        holder = jnp.zeros((ROWS, HD), jnp.int32)
        first_new = jnp.zeros((ROWS, HD), jnp.int32)
        stale = lane < 0
        for b in range(BW):
            near = parents_ref[1, p * BW + b]
            holder = jnp.where(row == b, parents_ref[0, p * BW + b] - p * BW, holder)
            holder = jnp.where(row == BW + b, parents_ref[0, near] - p * BW, holder)
            first_new = jnp.where(row == b, b, first_new)
            first_new = jnp.where(row == BW + b, near - p * BW, first_new)
            last_page = lax.rem(me - start_ref[0, p * BW + b] + 2 * CTX, CTX) == CTX - 1
            cut = jnp.where(last_page, PAGE - STEPS, PAGE)
            stale = stale | ((lane // PAGE == b) & (lane % PAGE >= cut))
        second_new = jnp.where(row < BW, first_new, row)
        old_seen = (lane // PAGE == holder) & jnp.logical_not(stale)
        owner = jnp.where(me == p * BW, 1, 0)
        new_seen = ((lane == first_new) | (lane == second_new)) & (owner == 1)

        old_bias = spread(jnp.where(old_seen, 0.0, -jnp.inf))
        new_bias = spread(jnp.where(new_seen, 0.0, -jnp.inf))
        s_pre = (
            lax.dot_general(query, prefix_ref[p, :, :HD], contract, preferred_element_type=F32)
            * scale
        )
        s_old = (
            lax.dot_general(query, tail[:, :HD], contract, preferred_element_type=F32) * scale
            + old_bias
        )
        s_new = (
            lax.dot_general(query, new_key, contract, preferred_element_type=F32) * scale
            + new_bias
        )
        peak = jnp.maximum(
            jnp.max(s_pre, axis=1, keepdims=True),
            jnp.max(jnp.maximum(s_old, s_new), axis=1, keepdims=True),
        )
        w_pre = jnp.exp(s_pre - peak)
        w_old = jnp.exp(s_old - peak)
        w_new = jnp.exp(s_new - peak)
        total = jnp.sum(w_pre, axis=1, keepdims=True) + jnp.sum(w_old + w_new, axis=1, keepdims=True)
        mixed = (
            jnp.dot(w_pre.astype(BF16), prefix_ref[p, :, HD:], preferred_element_type=F32)
            + jnp.dot(w_old.astype(BF16), tail[:, HD:], preferred_element_type=F32)
            + jnp.dot(w_new.astype(BF16), new_value, preferred_element_type=F32)
        )
        out_ref[p * GROUP : (p + 1) * GROUP, :ROWS, :] = mixed.astype(BF16).reshape(
            GROUP, ROWS, HD
        )

        def split(value):
            high = value.astype(BF16).astype(F32)
            rest = value - high
            mid = rest.astype(BF16).astype(F32)
            return high, mid, rest - mid

        table = jnp.zeros((GROUP * ROWS, HD), F32)
        for k, piece in enumerate(split(peak) + split(total)):
            table = jnp.where(lane_full == k, piece, table)
        stats = table.T[:8].astype(BF16)
        for h in range(GROUP):
            out_ref[p * GROUP + h, ROWS:, :] = stats


def merge_kernel(parts_ref, out_ref, scale_ref):
    h = lax.rem(lax.axis_index("ctx"), GROUP)
    stats = parts_ref[:, ROWS:, :].astype(F32)
    kind = lax.broadcasted_iota(jnp.int32, stats.shape, 1)
    peak = jnp.sum(jnp.where(kind < 3, stats, 0.0), axis=1)
    total = jnp.sum(jnp.where((kind >= 3) & (kind < 6), stats, 0.0), axis=1)
    factor = jnp.exp(peak - jnp.max(peak, axis=0, keepdims=True))
    factor = factor / jnp.sum(total * factor, axis=0, keepdims=True)
    factor = jnp.concatenate([factor, jnp.zeros((HD - CTX, HD), F32)], axis=0)
    scale_ref[...] = factor.T
    mine = scale_ref[pl.ds(pl.multiple_of(h * ROWS, ROWS), ROWS), :]
    acc = jnp.zeros((ROWS, HD), F32)
    for k in range(CTX):
        acc = acc + mine[:, k : k + 1] * parts_ref[k, :ROWS, :].astype(F32)
    out_ref[...] = jnp.broadcast_to(acc.astype(BF16)[None], out_ref.shape)


def output_kernel(heads_ref, weight_ref, out_ref):
    prompts = out_ref.shape[0]
    acc = jnp.zeros((prompts * ROWS, HD), F32)
    for h in range(GROUP):
        head = jnp.concatenate([heads_ref[p * GROUP + h] for p in range(prompts)], axis=0)
        acc = acc + jnp.dot(
            head, weight_ref[h * HD : (h + 1) * HD, :], preferred_element_type=F32
        )
    out_ref[...] = acc.astype(BF16).reshape(out_ref.shape)


def source_of(parents_ref, start_ref, c):
    far = parents_ref[0, parents_ref[1, c]]
    return far, lax.rem(start_ref[2, c] - start_ref[0, far] + CTX, CTX)


def pick_xc_kernel(parents_ref, start_ref, pages_ref, out_ref, sems):
    me = lax.axis_index("ctx")
    core, y, x = lax.rem(me, LC), lax.rem(me // LC, LY), me // (LC * LY)
    beams = out_ref.shape[0]

    def copy(c):
        far, shift = source_of(parents_ref, start_ref, c)
        s_core, s_y, s_x = lax.rem(shift, LC), lax.rem(shift // LC, LY), shift // (LC * LY)
        from_core = lax.rem(core - s_core + LC, LC)
        carry_y = (from_core + s_core) // LC
        carry_x = (y + s_y + carry_y) // LY
        from_x = lax.rem(x - s_x - carry_x + 2 * LX, LX)
        return pltpu.make_async_copy(
            pages_ref.at[(from_x * LC + from_core) * beams + far], out_ref.at[c], sems.at[c]
        )

    def start(c, _):
        copy(c).start()
        return 0

    def wait(c, _):
        pltpu.make_async_copy(pages_ref.at[0], out_ref.at[c], sems.at[c]).wait()
        return 0

    lax.fori_loop(0, beams, start, 0)
    lax.fori_loop(0, beams, wait, 0)


def finish_tail_kernel(parents_ref, start_ref, pages_ref, shared_ref, out_ref, fresh, sems):
    me = lax.axis_index("ctx")
    core, y = lax.rem(me, LC), lax.rem(me // LC, LY)
    beams = out_ref.shape[0]

    def start(c, _):
        _, shift = source_of(parents_ref, start_ref, c)
        s_core, s_y = lax.rem(shift, LC), lax.rem(shift // LC, LY)
        from_core = lax.rem(core - s_core + LC, LC)
        from_y = lax.rem(y - s_y - (from_core + s_core) // LC + 2 * LY, LY)
        pltpu.make_async_copy(
            pages_ref.at[from_y * beams + c], out_ref.at[c], sems.at[c]
        ).start()
        return 0

    def wait(c, _):
        pltpu.make_async_copy(pages_ref.at[0], out_ref.at[c], sems.at[c]).wait()
        return 0

    lax.fori_loop(0, beams, start, 0)
    for s in range(STEPS):
        for p in range(beams // BW):
            for kv in range(2):
                entry = shared_ref[p * GROUP + 2 * s + kv, ROWS:, :].astype(F32)
                fresh[s, p * BW : (p + 1) * BW, :, kv * HD : (kv + 1) * HD] = entry[:, None, :]
    lax.fori_loop(0, beams, wait, 0)

    def append(c, _):
        @pl.when(lax.rem(start_ref[2, c] - 1 + CTX, CTX) == me)
        def _():
            page = out_ref[c].astype(F32)
            line = lax.broadcasted_iota(jnp.int32, page.shape, 0)
            page = jnp.where(line == PAGE - 2, fresh[0, parents_ref[1, c]], page)
            page = jnp.where(line == PAGE - 1, fresh[1, c], page)
            out_ref[c] = page.astype(BF16)

        return 0

    lax.fori_loop(0, beams, append, 0)


def call(kernel, shape, in_specs, scratch=(), cost=None, dtype=BF16):
    return pl.pallas_call(
        kernel,
        out_shape=jax.ShapeDtypeStruct(shape, dtype),
        in_specs=in_specs,
        out_specs=VMEM,
        scratch_shapes=list(scratch),
        compiler_params=PARAMS,
        cost_estimate=cost,
    )


def per_device(
    hidden, qkv_weight, qkv_bias, out_weight, prefix_cache, tail_cache, parents, start_dev
):
    prompts = prefix_cache.shape[0]
    beams = prompts * BW
    pages = tail_cache.reshape(beams, PAGE, 2 * HD)
    cosine, sine = rope_rows()
    swap = functools.partial(lax.all_to_all, split_axis=0, concat_axis=0, tiled=True)

    wide = lax.all_gather(pages, "ctx", axis_index_groups=XC_GROUPS, tiled=True)

    parts = call(project_kernel, (CTX, PACK, HD), [VMEM] * 2)(hidden, qkv_weight)
    parts = swap(parts, "ctx")
    mine = call(rotate_kernel, (CTX, PACK, HD), [VMEM] * 4)(
        parts, qkv_bias.reshape(GROUP + 2, HD), cosine, sine
    )
    shared = swap(mine, "ctx")
    parts = call(attend_kernel, (CTX, PACK, HD), [SMEM] * 2 + [VMEM] * 3)(
        parents, start_dev, shared, prefix_cache, pages
    )
    parts, wide = lax.optimization_barrier((parts, wide))

    moved = call(
        pick_xc_kernel,
        (beams, PAGE, 2 * HD),
        [SMEM] * 2 + [ANY],
        [pltpu.SemaphoreType.DMA((beams,))],
    )(parents, start_dev, wide)
    deep = lax.all_gather(moved, "ctx", axis_index_groups=Y_GROUPS, tiled=True)

    parts = swap(parts, "ctx")
    merged = call(
        merge_kernel, (CTX, ROWS, HD), [VMEM], [pltpu.VMEM((HD, HD), F32)]
    )(parts)
    heads = swap(merged, "ctx")
    share = call(output_kernel, (prompts, ROWS, HD), [VMEM] * 2)(heads, out_weight)
    share = swap(share, "tp")
    share, deep = lax.optimization_barrier((share, deep))
    attended = jnp.sum(share.astype(F32), axis=0).astype(BF16).reshape(STEPS, BW, HD)
    tail_out = call(
        finish_tail_kernel,
        (beams, PAGE, 2 * HD),
        [SMEM] * 2 + [ANY, VMEM],
        [
            pltpu.VMEM((STEPS, beams, 1, 2 * HD), F32),
            pltpu.SemaphoreType.DMA((beams,)),
        ],
    )(parents, start_dev, deep, shared)
    return attended, tail_out.reshape(tail_cache.shape)


def solution(mesh):
    placed = (
        P(None, None, "ctx"),
        P("ctx", "tp"),
        P("tp"),
        P("tp", "ctx"),
        P(None, "ctx", "tp"),
        P("ctx", None, None, "tp"),
        P(),
        P(),
    )
    return jax.shard_map(
        per_device,
        mesh=mesh,
        in_specs=placed,
        out_specs=(P(None, "tp", "ctx"), P("ctx", None, None, "tp")),
        check_vma=False,
    )
```

time: 726 us -> 153 us (0.21); the launches traced: 714 us -> 153 us
  other arithmetic: 223 us -> 0.6 us
  waiting for transfers between devices: 197 us -> 2.65 us
  blocking collectives: 196 us -> 108 us
  local copies, waits for them, and re-layouts: 45.4 us -> 9.95 us
  starting transfers between devices: 20.1 us -> 0.08 us
  Pallas kernels: 0 us -> 17.6 us
  matrix products: 11.3 us -> 0 us
    psum x1 -> x0, waiting for transfers between devices: 197 us -> none  [per_device(): projected = lax.psum(partial_proj, 'ctx') + qkv_bias.astype(jnp.float32)]
    all_gather x4 -> x0, blocking collectives: 172 us -> none  [merged(): everything = jax.tree.map(lambda part: lax.all_gather(part, axis), shard)]
    add x129 -> x0, other arithmetic: 154 us -> none  [the longest x126 152 us: combine_parts(): mixed_one * scale_one[..., None] + mixed_two * scale_two[..., None]]
    all_to_all x0 -> x5, blocking collectives: none -> 108 us  [the longest x2 46.8 us: per_device(): parts = swap(parts, 'ctx')]
    mul x253 -> x0, other arithmetic: 47.2 us -> none  [the longest x126 44.9 us: combine_parts(): mixed_two * scale_two[..., None]]
    unnamed x1 -> x0, blocking collectives: 23.6 us -> none
    mul x252 -> x0, local copies, waits for them, and re-layouts: 21.2 us -> none  [the longest x126 10.6 us: combine_parts(): mixed_two * scale_two[..., None]]
    all_to_all x2 -> x0, starting transfers between devices: 19.9 us -> none  [per_device(): lax.all_to_all(send_rows, 'ctx', split_axis=0, concat_axis=0, tiled=True)]
  transfers between devices with their start and end apart: 5 -> 2, of which waited for: 1 -> 1; matrix products, arithmetic and copies ran while one was open for 23% -> 0% of each run, Pallas kernels for 0% -> 3%
where the time goes in v1:
time: 153 us
  blocking collectives  108 us (71%)
  Pallas kernels  17.6 us (12%)
  between operations  14.2 us (9%)
  local copies, waits for them, and re-layouts  9.95 us (7%)
  waiting for transfers between devices  2.65 us (2%)
    all_to_all x2, blocking collectives, per_device(): parts = swap(parts, 'ctx')  46.8 us
    all_to_all x1, blocking collectives, per_device(): heads = swap(merged, 'ctx')  21.3 us
    all_to_all x1, blocking collectives, per_device(): shared = swap(mine, 'ctx')  20.6 us
    all_to_all x1, blocking collectives, per_device(): share = swap(share, 'tp')  19.1 us
    unnamed x28, local copies, waits for them, and re-layouts  9.95 us
    pallas_call x1, Pallas kernels, per_device(): call(finish_tail_kernel, (beams, PAGE, 2 * HD), [SMEM] * 2 + [ANY, VMEM],...  6.88 us
    pallas_call x1, Pallas kernels, per_device(): call(pick_xc_kernel, (beams, PAGE, 2 * HD), [SMEM] * 2 + [ANY], [pltpu.Se...  6.2 us
    pallas_call x1, Pallas kernels, per_device(): call(attend_kernel, (CTX, PACK, HD), [SMEM] * 2 + [VMEM] * 3)  3.23 us
  transfers between devices with their start and end apart: 2, of which 1 were waited for; matrix products, arithmetic and copies ran while one was open for 0% of the time, Pallas kernels for 3%

profile of v1, /device:TPU:1, one launch (start us, length us, event | category | flops | bytes accessed | tf_op | source)
XLA Modules:
  0.0 152.8 jit_solution(15224865643451773842)
XLA Ops:
  7.2 0.0 copy-start.2
  7.2 0.0 copy-start.3
  7.2 0.0 all-gather.6.cloned.1.call-start
  7.2 0.7 all-gather.6.cloned.1.call-update
  7.9 0.0 all-gather.4.cloned.1.call-start
  8.0 0.0 copy-start.4
  8.0 1.0 copy-done.4
  8.9 0.0 copy-start.8
  8.9 0.8 copy-done.8
  9.7 0.0 copy-start.10
  9.7 0.0 copy-start.12
  9.7 0.2 shard_map.113
  9.9 26.0 %all_to_all.25.parts_ref = bf16[64,24,128]{2,1,0:T(8,128)(2,1)S(1)} all-to-all(bf16[64,24,128]{2,1,0:T(8,128)(2,1)S(1)} %shard_map.113), channel_id=1, replica_groups=mesh['ctx'=64,'tp'=8] {'ctx'}, dimensions={0} | all-to-all | bytes 786432 | tf_op jit(solution)/shard_map/all_to_all | solution.py:301
  36.0 0.0 copy-start.6
  36.0 0.9 copy-done.6
  36.9 0.0 copy-start.7
  36.9 0.9 copy-done.7
  37.8 0.0 copy-start.13
  37.8 0.7 copy-done.13
  38.5 0.2 shard_map.114
  38.6 20.6 %all_to_all.26.shared_ref = bf16[64,24,128]{2,1,0:T(8,128)(2,1)S(1)} all-to-all(bf16[64,24,128]{2,1,0:T(8,128)(2,1)S(1)} %shard_map.114), channel_id=1, replica_groups=mesh['ctx'=64,'tp'=8] {'ctx'}, dimensions={0} | all-to-all | bytes 786432 | tf_op jit(solution)/shard_map/all_to_all | solution.py:305
  59.3 0.0 copy-done.2
  59.3 0.0 copy-done.3
  59.3 0.0 copy-start.9
  59.3 0.7 copy-done.9
  60.0 0.0 copy-start.11
  60.0 0.7 copy-done.11
  60.6 0.0 copy-start.5
  60.6 3.2 %shard_map.115 = bf16[64,24,128]{2,1,0:T(8,128)(2,1)S(1)} custom-call(s32[2,64]{1,0:T(2,128)S(1)} %copy-done.11, s32[3,64]{1,0:T(4,128)S(1)} %copy-done.9, bf16[64,24,128]{2,1,0:T(8,128)(2,1)S(1)} %all_to_all.26.shared_ref, bf16[8,256,256]{2,1,0:T(8,128)(2,1)S(1)} %copy-done.3, bf16[64,16,256]{2,1,0:T(8,128)(2,1)S(1)} %bitcast.8), custom_call_target="tpu_custom_call" | custom-call | tf_op jit(solution)/shard_map/pallas_call | solution.py:306
  63.9 0.0 all-gather.6.cloned.1.call-done
  63.9 0.0 copy-done.10
  63.9 0.0 copy-done.12
  63.9 0.0 copy-start
  63.9 2.2 %copy-done = bf16[512,1,16,256]{3,2,1,0:T(8,128)(2,1)S(1)} copy-done((bf16[512,1,16,256]{3,2,1,0:T(8,128)(2,1)S(1)}, bf16[512,1,16,256]{3,2,1,0:T(8,128)(2,1)}, u32[]{:S(2)}) %copy-start) | copy-done | bytes 4194328
  66.1 6.2 %shard_map.118 = bf16[64,16,256]{2,1,0:T(8,128)(2,1)} custom-call(s32[2,64]{1,0:T(2,128)S(1)} %copy-done.12, s32[3,64]{1,0:T(4,128)S(1)} %copy-done.10, bf16[512,16,256]{2,1,0:T(8,128)(2,1)S(1)} %bitcast.7), custom_call_target="tpu_custom_call" | custom-call | tf_op jit(solution)/shard_map/pallas_call | solution.py:311
  72.3 0.0 all-gather.4.cloned.1.call-update
  72.3 20.7 %all_to_all.27.parts_ref = bf16[64,24,128]{2,1,0:T(8,128)(2,1)S(1)} all-to-all(bf16[64,24,128]{2,1,0:T(8,128)(2,1)S(1)} %shard_map.115), channel_id=1, replica_groups=mesh['ctx'=64,'tp'=8] {'ctx'}, dimensions={0} | all-to-all | bytes 786432 | tf_op jit(solution)/shard_map/all_to_all | solution.py:319
  93.1 0.6 shard_map.116
  93.7 21.3 %all_to_all.28.heads_ref = bf16[64,16,128]{2,1,0:T(8,128)(2,1)S(1)} all-to-all(bf16[64,16,128]{2,1,0:T(8,128)(2,1)S(1)} %shard_map.116), channel_id=1, replica_groups=mesh['ctx'=64,'tp'=8] {'ctx'}, dimensions={0} | all-to-all | bytes 524288 | tf_op jit(solution)/shard_map/all_to_all | solution.py:323
  115.0 0.0 copy-done.5
  115.0 0.2 shard_map.117
  115.2 19.1 %all_to_all.29 = bf16[8,16,128]{2,1,0:T(8,128)(2,1)S(1)} all-to-all(bf16[8,16,128]{2,1,0:T(8,128)(2,1)S(1)} %shard_map.117), channel_id=1, replica_groups=mesh['ctx'=64,'tp'=8] {'tp'}, dimensions={0} | all-to-all | bytes 65536 | tf_op jit(solution)/shard_map/all_to_all | solution.py:325
  134.3 1.9 %all-gather.4.cloned.1.call-done.pages_ref = bf16[512,16,256]{2,1,0:T(8,128)(2,1)} async-done(((bf16[64,16,256]{2,1,0:T(8,128)(2,1)}), bf16[512,16,256]{2,1,0:T(8,128)(2,1)}) %all-gather.4.cloned.1.call-update) | async-done | bytes 4194320 | tf_op jit(solution)/shard_map/all_gather | solution.py:317
  136.3 0.6 reduce_sum.12
  136.9 0.0 copy-start.1
  136.9 2.2 %copy-done.1 = bf16[512,16,256]{2,1,0:T(8,128)(2,1)S(1)} copy-done((bf16[512,16,256]{2,1,0:T(8,128)(2,1)S(1)}, bf16[512,16,256]{2,1,0:T(8,128)(2,1)}, u32[]{:S(2)}) %copy-start.1) | copy-done | bytes 4194328
  139.0 6.9 %shard_map.119 = bf16[64,16,256]{2,1,0:T(8,128)(2,1)} custom-call(s32[2,64]{1,0:T(2,128)S(1)} %copy-done.12, s32[3,64]{1,0:T(4,128)S(1)} %copy-done.10, bf16[512,16,256]{2,1,0:T(8,128)(2,1)S(1)} %copy-done.1, bf16[64,24,128]{2,1,0:T(8,128)(2,1)S(1)} %all_to_all.26.shared_ref), custom_call_target="tpu_custom_call" | custom-call | tf_op jit(solution)/shard_map/pallas_call | solution.py:328
Async XLA Ops:
  7.2 52.1 %copy-start.2 = (bf16[64,1,16,256]{3,2,1,0:T(8,128)(2,1)S(1)}, bf16[64,1,16,256]{3,2,1,0:T(8,128)(2,1)}, u32[]{:S(2)}) copy-start(bf16[64,1,16,256]{3,2,1,0:T(8,128)(2,1)} %param.15) | copy-start | bytes 1572868
  7.2 52.1 %copy-start.3 = (bf16[8,256,256]{2,1,0:T(8,128)(2,1)S(1)}, bf16[8,256,256]{2,1,0:T(8,128)(2,1)}, u32[]{:S(2)}) copy-start(bf16[8,256,256]{2,1,0:T(8,128)(2,1)} %prefix_ref.1) | copy-start | bytes 3145732
  7.2 56.7 %all-gather.6.cloned.1.call-start = ((), (), s32[]{:S(2)}) async-start(), calls=%async_computation.6 | async-start | bytes 4718592 | tf_op jit(solution)/shard_map/all_gather | solution.py:298
  7.9 128.3 %all-gather.4.cloned.1.call-start = ((), (), s32[]{:S(2)}) async-start(), calls=%async_computation.5 | async-start | bytes 4718592 | tf_op jit(solution)/shard_map/all_gather | solution.py:317
  8.0 1.0 copy-start.4
  8.9 0.8 copy-start.8
  9.7 54.2 %copy-start.10 = (s32[3,64]{1,0:T(4,128)S(1)}, s32[3,64]{1,0:T(4,128)}, u32[]{:S(2)}) copy-start(s32[3,64]{1,0:T(4,128)} %start_ref.5) | copy-start | bytes 2308
  9.7 54.2 %copy-start.12 = (s32[2,64]{1,0:T(2,128)S(1)}, s32[2,64]{1,0:T(2,128)}, u32[]{:S(2)}) copy-start(s32[2,64]{1,0:T(2,128)} %parents_ref.5) | copy-start | bytes 1540
  36.0 0.9 copy-start.6
  36.9 0.9 copy-start.7
  37.8 0.7 copy-start.13
  59.3 0.7 copy-start.9
  60.0 0.7 copy-start.11
  60.6 54.4 %copy-start.5 = (bf16[1024,128]{1,0:T(8,128)(2,1)S(1)}, bf16[1024,128]{1,0:T(8,128)(2,1)}, u32[]{:S(2)}) copy-start(bf16[1024,128]{1,0:T(8,128)(2,1)} %weight_ref.3) | copy-start | bytes 786436
  63.9 2.2 %copy-start = (bf16[512,1,16,256]{3,2,1,0:T(8,128)(2,1)S(1)}, bf16[512,1,16,256]{3,2,1,0:T(8,128)(2,1)}, u32[]{:S(2)}) copy-start(bf16[512,1,16,256]{3,2,1,0:T(8,128)(2,1)} %all-gather.6.cloned.1.call-done) | copy-start | bytes 12582916
  136.9 2.2 %copy-start.1 = (bf16[512,16,256]{2,1,0:T(8,128)(2,1)S(1)}, bf16[512,16,256]{2,1,0:T(8,128)(2,1)}, u32[]{:S(2)}) copy-start(bf16[512,16,256]{2,1,0:T(8,128)(2,1)} %all-gather.4.cloned.1.call-done.pages_ref) | copy-start | bytes 12582916
Sparse Core Ops, SparseCore 0:
  10.2 45.3 all-gather.5
  72.5 63.7 all-gather.3

commit v2 on v1

v2 whole, which is shorter than its diff:
```python
import functools

import jax
import jax.numpy as jnp
import numpy as np
from jax import lax
from jax.experimental import pallas as pl
from jax.experimental.pallas import tpu as pltpu
from jax.sharding import PartitionSpec as P

HD = 128
BW = 8
GROUP = 8
STEPS = 2
ROWS = STEPS * BW
PAGE = 16
CTX = 64
POSITION = 17406
MIB = 1024 * 1024
F32, BF16 = jnp.float32, jnp.bfloat16

KEYS_AT, VALUES_AT, FRESH_AT, SENT = ROWS, ROWS + PAGE, ROWS + 2 * PAGE, ROWS + 2 * PAGE + BW
PACK = ROWS + 8
CARRY = ROWS + 2 * PAGE

VMEM = pl.BlockSpec(memory_space=pltpu.VMEM)
SMEM = pl.BlockSpec(memory_space=pltpu.SMEM)
HBM = pl.BlockSpec(memory_space=pltpu.HBM)


def rope_rows():
    half = HD // 2
    frequency = 1000000.0 ** (-(np.arange(half) * 2.0) / HD)
    table = np.zeros((8, HD), np.float32)
    for s in range(STEPS):
        angles = (POSITION + s) * frequency
        table[s] = np.concatenate([np.cos(angles), np.cos(angles)])
        table[STEPS + s] = np.concatenate([-np.sin(angles), np.sin(angles)])
    return table


def iota(shape, dim):
    return lax.broadcasted_iota(jnp.int32, shape, dim)


def project_kernel(
    parents_ref,
    start_ref,
    hidden_hbm,
    weight_hbm,
    bias_hbm,
    table_hbm,
    pages_hbm,
    out_ref,
    seen_ref,
    hidden_ref,
    weight_ref,
    bias_ref,
    table_ref,
    pages_ref,
    sems,
):
    me = lax.axis_index("ctx")
    pairs = (
        (hidden_hbm, hidden_ref),
        (weight_hbm, weight_ref),
        (bias_hbm, bias_ref),
        (table_hbm, table_ref),
        (pages_hbm, pages_ref),
    )
    copies = [pltpu.make_async_copy(a, b, sems.at[k]) for k, (a, b) in enumerate(pairs)]
    for copy in copies:
        copy.start()
    prompts = hidden_ref.shape[1] // BW
    beams = prompts * BW
    lane = iota((ROWS, HD), 1)
    row = iota((ROWS, HD), 0)

    for p in range(prompts):
        holder = jnp.zeros((ROWS, HD), jnp.int32)
        stale = lane < 0
        for b in range(BW):
            near = parents_ref[1, p * BW + b]
            holder = jnp.where(row == b, parents_ref[0, p * BW + b] - p * BW, holder)
            holder = jnp.where(row == BW + b, parents_ref[0, near] - p * BW, holder)
            last_page = ((me - start_ref[0, p * BW + b]) & (CTX - 1)) == CTX - 1
            cut = jnp.where(last_page, PAGE - STEPS, PAGE)
            stale = stale | ((lane // PAGE == b) & (lane % PAGE >= cut))
        old_seen = (lane // PAGE == holder) & jnp.logical_not(stale)
        seen_ref[p] = jnp.where(old_seen, 0.0, -jnp.inf)

    base = (me >> 3) * BW
    first_new = jnp.zeros((ROWS, HD), jnp.int32)
    for b in range(BW):
        first_new = jnp.where(row == b, b, first_new)
        first_new = jnp.where(row == BW + b, parents_ref[1, base + b] - base, first_new)
    second_new = jnp.where(row < BW, first_new, row)
    seen_ref[prompts] = jnp.where((lane == first_new) | (lane == second_new), 0.0, -jnp.inf)

    near = parents_ref[1, me]
    shift = (start_ref[2, me] - start_ref[0, parents_ref[0, near]]) & (CTX - 1)
    last = (start_ref[2, me] - 1) & (CTX - 1)
    facts = jnp.where(row == 0, shift, jnp.where(row == 1, last, near - base))
    seen_ref[prompts + 1] = facts.astype(F32)

    for copy in copies:
        copy.wait()
    for c in range(beams):
        far = parents_ref[0, parents_ref[1, c]]
        out_ref[c, KEYS_AT:VALUES_AT, :] = pages_ref[far, :, :HD]
        out_ref[c, VALUES_AT:FRESH_AT, :] = pages_ref[far, :, HD:]

    cosine = [jnp.broadcast_to(table_ref[s : s + 1], (BW, HD)) for s in range(STEPS)]
    sine = [jnp.broadcast_to(table_ref[STEPS + s : STEPS + s + 1], (BW, HD)) for s in range(STEPS)]
    cosine = jnp.concatenate(cosine * prompts, axis=0)
    sine = jnp.concatenate(sine * prompts, axis=0)
    steps = [hidden_ref[s].astype(F32) for s in range(STEPS)]
    rows = [steps[s][p * BW : (p + 1) * BW] for p in range(prompts) for s in range(STEPS)]
    hidden = jnp.concatenate(rows, axis=0).astype(BF16)
    bias = bias_ref[...].astype(F32) * (1.0 / CTX)
    for col in range(GROUP + 2):
        part = jnp.dot(
            hidden, weight_ref[:, col * HD : (col + 1) * HD], preferred_element_type=F32
        )
        part = part + bias[col : col + 1]
        if col <= GROUP:
            part = part * cosine + pltpu.roll(part, HD // 2, 1) * sine
        for p in range(prompts):
            tile = part[p * ROWS : (p + 1) * ROWS]
            if col < GROUP:
                out_ref[p * GROUP + col, :ROWS, :] = tile.astype(BF16)
            else:
                for h in range(GROUP):
                    if h % 2 == col - GROUP:
                        s = h // 2 % 2
                        out_ref[p * GROUP + h, FRESH_AT:, :] = tile[s * BW : (s + 1) * BW].astype(
                            BF16
                        )


def sum_kernel(parts_ref, out_ref, own_ref):
    query = jnp.sum(parts_ref[:, :ROWS, :].astype(F32), axis=0).astype(BF16)
    fresh = jnp.sum(parts_ref[:, FRESH_AT:, :].astype(F32), axis=0).astype(BF16)
    out_ref[...] = jnp.broadcast_to(query[None], out_ref.shape)
    own_ref[:ROWS, :] = query
    own_ref[ROWS:, :] = fresh


def attend_kernel(shared_ref, prefix_ref, pages_ref, seen_ref, own_ref, out_ref):
    h_me = lax.axis_index("ctx") & (GROUP - 1)
    prompts = prefix_ref.shape[0]
    scale = HD**-0.5
    contract = (((1,), (1,)), ((), ()))
    lane = iota((GROUP * ROWS, HD), 1)
    row = iota((GROUP * ROWS, HD), 0)
    slot = lane // ROWS
    diagonal = lane % ROWS == row % ROWS

    fresh = own_ref[ROWS:, :].astype(F32)
    fresh = jnp.where(h_me < GROUP // 2, pltpu.roll(fresh, 4, 0), fresh)
    line = iota((8, HD), 0)
    fresh = jnp.where(line >= 4, fresh, 0.0)

    def split(value):
        high = value.astype(BF16).astype(F32)
        rest = value - high
        mid = rest.astype(BF16).astype(F32)
        return high, mid, rest - mid

    for p in range(prompts):
        query = shared_ref[p * GROUP : (p + 1) * GROUP].reshape(GROUP * ROWS, HD)
        tail = pages_ref[p * BW : (p + 1) * BW].reshape(BW * PAGE, 2 * HD)
        s_pre = (
            lax.dot_general(query, prefix_ref[p, :, :HD], contract, preferred_element_type=F32)
            * scale
        )
        s_old = lax.dot_general(
            query, tail[:, :HD], contract, preferred_element_type=F32
        ) * scale + jnp.concatenate([seen_ref[p]] * GROUP, axis=0)
        peak = jnp.maximum(
            jnp.max(s_pre, axis=1, keepdims=True), jnp.max(s_old, axis=1, keepdims=True)
        )
        w_pre = jnp.exp(s_pre - peak)
        w_old = jnp.exp(s_old - peak)
        total = jnp.sum(w_pre, axis=1, keepdims=True) + jnp.sum(w_old, axis=1, keepdims=True)
        mixed = jnp.dot(
            w_pre.astype(BF16), prefix_ref[p, :, HD:], preferred_element_type=F32
        ) + jnp.dot(w_old.astype(BF16), tail[:, HD:], preferred_element_type=F32)
        out_ref[p * GROUP : (p + 1) * GROUP, :ROWS, :] = mixed.astype(BF16).reshape(
            GROUP, ROWS, HD
        )
        table = jnp.zeros((GROUP * ROWS, HD), F32)
        for k, term in enumerate(split(peak) + split(total)):
            table = jnp.where(slot == k, term, table)
        table = jnp.sum(jnp.where(diagonal, table, 0.0).reshape(GROUP, ROWS, HD), axis=1)
        for h in range(GROUP):
            out_ref[p * GROUP + h, ROWS:, :] = jnp.where(
                line == 0, table[h : h + 1], fresh
            ).astype(BF16)


def merge_kernel(parts_ref, own_ref, seen_ref, first_ref, out_ref):
    me = lax.axis_index("ctx")
    base = (me >> 3) * GROUP
    prompts = seen_ref.shape[0] - 2
    line = iota((8, HD), 0)

    def gather(kv):
        tiles = []
        for s in range(STEPS):
            low = parts_ref[base + 2 * s + kv, ROWS:, :].astype(F32)
            high = parts_ref[base + 2 * s + kv + GROUP // 2, ROWS:, :].astype(F32)
            tiles.append(jnp.where(line < 4, pltpu.roll(low, 4, 0), high))
        return tiles

    new_keys, new_values = gather(0), gather(1)
    blank = [jnp.zeros((HD - ROWS, HD), F32)]
    key = jnp.concatenate(new_keys + blank, axis=0).astype(BF16)
    value = jnp.concatenate(new_values + blank, axis=0).astype(BF16)
    s_new = (
        lax.dot_general(
            own_ref[:ROWS, :], key, (((1,), (1,)), ((), ())), preferred_element_type=F32
        )
        * HD**-0.5
        + seen_ref[prompts]
    )

    stats = parts_ref[:, ROWS:, :].astype(F32)
    stats = jnp.sum(jnp.where(iota(stats.shape, 1) == 0, stats, 0.0), axis=1)

    def term(k):
        return stats if k == 0 else pltpu.roll(stats, HD - k * ROWS, 1)

    def upright(table):
        return jnp.concatenate([table, jnp.zeros((HD - CTX, HD), F32)], axis=0).T[:ROWS]

    peak = upright(term(0) + term(1) + term(2))
    total = upright(term(3) + term(4) + term(5))
    peak = jnp.where(iota((ROWS, HD), 1) < CTX, peak, -jnp.inf)
    top = jnp.maximum(
        jnp.max(peak, axis=1, keepdims=True), jnp.max(s_new, axis=1, keepdims=True)
    )
    factor = jnp.exp(peak - top)
    w_new = jnp.exp(s_new - top)
    denominator = jnp.sum(total * factor + w_new, axis=1, keepdims=True)
    acc = jnp.dot(w_new.astype(BF16), value, preferred_element_type=F32)
    for k in range(CTX):
        acc = acc + factor[:, k : k + 1] * parts_ref[k, :ROWS, :].astype(F32)
    attention = (acc / denominator).astype(BF16)

    facts = seen_ref[prompts + 1]
    shift = jnp.max(facts[0:1]).astype(jnp.int32)
    last = jnp.max(facts[1:2]).astype(jnp.int32)
    for k in range(CTX):
        out_ref[k, :ROWS, :] = attention
        out_ref[k, ROWS:, :] = first_ref[(k - shift) & (CTX - 1), KEYS_AT:FRESH_AT, :]

    mine = (me & (BW - 1)).astype(F32)
    place = line.astype(F32)
    row = iota((PAGE, HD), 0)
    for at, tiles in ((ROWS, new_keys), (ROWS + PAGE, new_values)):
        earlier = jnp.sum(jnp.where(place == facts[2:3], tiles[0], 0.0), axis=0, keepdims=True)
        newest = jnp.sum(jnp.where(place == mine, tiles[1], 0.0), axis=0, keepdims=True)
        page = out_ref[last, at : at + PAGE, :].astype(F32)
        page = jnp.where(row == PAGE - 2, earlier, page)
        page = jnp.where(row == PAGE - 1, newest, page)
        out_ref[last, at : at + PAGE, :] = page.astype(BF16)


def output_kernel(heads_ref, weight_ref, out_ref):
    prompts = out_ref.shape[0]
    acc = jnp.zeros((prompts * ROWS, HD), F32)
    for h in range(GROUP):
        head = jnp.concatenate([heads_ref[p * GROUP + h, :ROWS, :] for p in range(prompts)], axis=0)
        acc = acc + jnp.dot(
            head, weight_ref[h * HD : (h + 1) * HD, :], preferred_element_type=F32
        )
    out_ref[...] = acc.astype(BF16).reshape(out_ref.shape)


def finish_kernel(share_ref, heads_hbm, out_ref, tail_hbm, sems):
    copies = [
        pltpu.make_async_copy(
            heads_hbm.at[:, pl.ds(ROWS + k * PAGE, PAGE), :],
            tail_hbm.at[:, :, pl.ds(k * HD, HD)],
            sems.at[k],
        )
        for k in range(2)
    ]
    for copy in copies:
        copy.start()
    total = jnp.sum(share_ref[...].astype(F32), axis=0)
    for s in range(STEPS):
        out_ref[s] = total[s * BW : (s + 1) * BW].astype(BF16)
    for copy in copies:
        copy.wait()


def call(kernel, shapes, in_specs, scratch=(), limit=32, out_specs=None):
    outs = [jax.ShapeDtypeStruct(shape, dtype) for shape, dtype in shapes]
    return pl.pallas_call(
        kernel,
        out_shape=outs,
        in_specs=in_specs,
        out_specs=out_specs or [VMEM] * len(outs),
        scratch_shapes=list(scratch),
        compiler_params=pltpu.CompilerParams(vmem_limit_bytes=limit * MIB),
    )


def per_device(
    hidden, qkv_weight, qkv_bias, out_weight, prefix_cache, tail_cache, parents, start_dev
):
    prompts = prefix_cache.shape[0]
    beams = prompts * BW
    pages = tail_cache.reshape(beams, PAGE, 2 * HD)
    bias = qkv_bias.reshape(GROUP + 2, HD)
    table = rope_rows()
    swap = functools.partial(lax.all_to_all, split_axis=0, concat_axis=0, tiled=True)

    parts, seen = call(
        project_kernel,
        [((CTX, SENT, HD), BF16), ((prompts + 2, ROWS, HD), F32)],
        [SMEM] * 2 + [HBM] * 5,
        [
            pltpu.VMEM(hidden.shape, BF16),
            pltpu.VMEM(qkv_weight.shape, BF16),
            pltpu.VMEM(bias.shape, BF16),
            pltpu.VMEM(table.shape, F32),
            pltpu.VMEM(pages.shape, BF16),
            pltpu.SemaphoreType.DMA((5,)),
        ],
        limit=60,
    )(parents, start_dev, hidden, qkv_weight, bias, table, pages)
    first = swap(parts, "ctx")
    mine, own = call(
        sum_kernel, [((CTX, ROWS, HD), BF16), ((ROWS + BW, HD), BF16)], [VMEM]
    )(first)
    shared = swap(mine, "ctx")
    (parts,) = call(attend_kernel, [((CTX, PACK, HD), BF16)], [VMEM] * 5)(
        shared, prefix_cache, pages, seen, own
    )
    parts = swap(parts, "ctx")
    (merged,) = call(merge_kernel, [((CTX, CARRY, HD), BF16)], [VMEM] * 4)(
        parts, own, seen, first
    )
    heads = swap(merged, "ctx")
    (share,) = call(output_kernel, [((prompts, ROWS, HD), BF16)], [VMEM] * 2)(heads, out_weight)
    share = swap(share, "tp")
    attended, tail_out = call(
        finish_kernel,
        [((STEPS, BW, HD), BF16), ((beams, PAGE, 2 * HD), BF16)],
        [VMEM, HBM],
        [pltpu.SemaphoreType.DMA((2,))],
        out_specs=[VMEM, HBM],
    )(share, heads)
    return attended, tail_out.reshape(tail_cache.shape)


def solution(mesh):
    placed = (
        P(None, None, "ctx"),
        P("ctx", "tp"),
        P("tp"),
        P("tp", "ctx"),
        P(None, "ctx", "tp"),
        P("ctx", None, None, "tp"),
        P(),
        P(),
    )
    return jax.shard_map(
        per_device,
        mesh=mesh,
        in_specs=placed,
        out_specs=(P(None, "tp", "ctx"), P("ctx", None, None, "tp")),
        check_vma=False,
    )
```

time: 153 us -> 131 us (0.86)
  blocking collectives: 108 us -> 122 us
  between operations: 14.2 us -> 0.69 us
  local copies, waits for them, and re-layouts: 9.95 us -> 0.02 us
  Pallas kernels: 17.6 us -> 8.06 us
  waiting for transfers between devices: 2.65 us -> 0 us
    all_to_all x0 -> x1, blocking collectives: none -> 37.5 us  [per_device(): first = swap(parts, 'ctx')]
    all_to_all x2 -> x1, blocking collectives: 46.8 us -> 20.4 us  [per_device(): parts = swap(parts, 'ctx')]
    unnamed x28 -> x8, local copies, waits for them, and re-layouts: 9.95 us -> 0.02 us
    pallas_call x7 -> x6, Pallas kernels: 17.6 us -> 8.06 us  [the longest x1 3.35 us: per_device(): call(project_kernel, [((CTX, SENT, HD), BF16), ((prompts + 2, ROWS, HD),...]
    all_to_all x1, blocking collectives: 21.3 us -> 29.1 us  [per_device(): heads = swap(merged, 'ctx')]
    all_to_all x1, blocking collectives: 20.6 us -> 18.1 us  [per_device(): shared = swap(mine, 'ctx')]
    all_to_all x1, blocking collectives: 19.1 us -> 16.8 us  [per_device(): share = swap(share, 'tp')]
    all_gather x2 -> x0, waiting for transfers between devices: 1.96 us -> none  [the longest x1 1.95 us: per_device(): deep = lax.all_gather(moved, 'ctx', axis_index_groups=Y_GROUPS, tiled=True)]
  transfers between devices with their start and end apart: 2 -> 0, of which waited for: 1 -> 0; matrix products, arithmetic and copies ran while one was open for 0% -> 0% of each run, Pallas kernels for 3% -> 0%
where the time goes in v2:
time: 131 us
  blocking collectives  122 us (93%)
  Pallas kernels  8.06 us (6%)
    all_to_all x1, blocking collectives, per_device(): first = swap(parts, 'ctx')  37.5 us
    all_to_all x1, blocking collectives, per_device(): heads = swap(merged, 'ctx')  29.1 us
    all_to_all x1, blocking collectives, per_device(): parts = swap(parts, 'ctx')  20.4 us
    all_to_all x1, blocking collectives, per_device(): shared = swap(mine, 'ctx')  18.1 us
    all_to_all x1, blocking collectives, per_device(): share = swap(share, 'tp')  16.8 us
    pallas_call x1, Pallas kernels, per_device(): call(project_kernel, [((CTX, SENT, HD), BF16), ((prompts + 2, ROWS, HD),...  3.35 us

profile of v2, /device:TPU:1, one launch (start us, length us, event | category | flops | bytes accessed | tf_op | source)
XLA Modules:
  0.0 130.8 jit_solution(15525182072509524348)
XLA Ops:
  0.6 3.4 %shard_map.104 = (bf16[64,56,128]{2,1,0:T(8,128)(2,1)}, f32[10,16,128]{2,1,0:T(8,128)}) custom-call(s32[2,64]{1,0:T(2,128)} %parents_ref.1, s32[3,64]{1,0:T(4,128)} %start_ref.1, bf16[2,64,128]{2,1,0:T(8,128)(2,1)} %hidden_hbm.1, bf16[128,1280]{1,0:T(8,128)(2,1)} %weight_hbm.1, bf16[10,128]{1,0:T(8,128)(2,1)} %bitcast.7, f32[8,128]{1,0:T(8,128)} %constant.2.clone.table_hbm, ...), custom_call_target="tpu_custom_call" | custom-call | tf_op jit(solution)/shard_map/pallas_call | solution.py:321
  4.0 0.0 copy-start.1
  4.0 37.5 %all_to_all.25.parts_ref.first_ref = bf16[64,56,128]{2,1,0:T(8,128)(2,1)S(1)} all-to-all(bf16[64,56,128]{2,1,0:T(8,128)(2,1)} %get-tuple-element.8), channel_id=1, replica_groups=mesh['ctx'=64,'tp'=8] {'ctx'}, dimensions={0} | all-to-all | bytes 1835008 | tf_op jit(solution)/shard_map/all_to_all | solution.py:335
  41.5 0.0 copy-start
  41.5 0.1 shard_map.105
  41.6 0.0 copy-start.2
  41.6 18.1 %all_to_all.26.shared_ref = bf16[64,16,128]{2,1,0:T(8,128)(2,1)S(1)} all-to-all(bf16[64,16,128]{2,1,0:T(8,128)(2,1)S(1)} %get-tuple-element.9), channel_id=1, replica_groups=mesh['ctx'=64,'tp'=8] {'ctx'}, dimensions={0} | all-to-all | bytes 524288 | tf_op jit(solution)/shard_map/all_to_all | solution.py:339
  59.8 0.0 copy-done.1
  59.8 0.0 copy-done
  59.8 0.0 copy-done.2
  59.8 2.3 %shard_map.106 = bf16[64,24,128]{2,1,0:T(8,128)(2,1)S(1)} custom-call(bf16[64,16,128]{2,1,0:T(8,128)(2,1)S(1)} %all_to_all.26.shared_ref, bf16[8,256,256]{2,1,0:T(8,128)(2,1)S(1)} %copy-done.1, bf16[64,16,256]{2,1,0:T(8,128)(2,1)S(1)} %bitcast.6, f32[10,16,128]{2,1,0:T(8,128)S(1)} %copy-done.2, bf16[24,128]{1,0:T(8,128)(2,1)S(1)} %get-tuple-element.11.own_ref), custom_call_target="tpu_custom_call" | custom-call | tf_op jit(solution)/shard_map/pallas_call | solution.py:340
  62.1 20.4 %all_to_all.27.parts_ref = bf16[64,24,128]{2,1,0:T(8,128)(2,1)S(1)} all-to-all(bf16[64,24,128]{2,1,0:T(8,128)(2,1)S(1)} %shard_map.106), channel_id=1, replica_groups=mesh['ctx'=64,'tp'=8] {'ctx'}, dimensions={0} | all-to-all | bytes 786432 | tf_op jit(solution)/shard_map/all_to_all | solution.py:343
  82.6 0.7 shard_map.107
  83.2 0.0 copy-start.3
  83.2 29.1 %all_to_all.28.heads_ref.heads_hbm = bf16[64,48,128]{2,1,0:T(8,128)(2,1)S(1)} all-to-all(bf16[64,48,128]{2,1,0:T(8,128)(2,1)S(1)} %shard_map.107), channel_id=1, replica_groups=mesh['ctx'=64,'tp'=8] {'ctx'}, dimensions={0} | all-to-all | bytes 1572864 | tf_op jit(solution)/shard_map/all_to_all | solution.py:347
  112.4 0.0 copy-done.3
  112.4 0.2 shard_map.108
  112.6 16.8 %all_to_all.29.share_ref = bf16[8,16,128]{2,1,0:T(8,128)(2,1)S(1)} all-to-all(bf16[8,16,128]{2,1,0:T(8,128)(2,1)S(1)} %shard_map.108), channel_id=1, replica_groups=mesh['ctx'=64,'tp'=8] {'tp'}, dimensions={0} | all-to-all | bytes 65536 | tf_op jit(solution)/shard_map/all_to_all | solution.py:349
  129.4 1.4 %shard_map.109 = (bf16[2,8,128]{2,1,0:T(8,128)(2,1)}, bf16[64,16,256]{2,1,0:T(8,128)(2,1)}) custom-call(bf16[8,16,128]{2,1,0:T(8,128)(2,1)S(1)} %all_to_all.29.share_ref, bf16[64,48,128]{2,1,0:T(8,128)(2,1)S(1)} %all_to_all.28.heads_ref.heads_hbm), custom_call_target="tpu_custom_call" | custom-call | tf_op jit(solution)/shard_map/pallas_call | solution.py:350
Async XLA Ops:
  4.0 55.8 %copy-start.1 = (bf16[8,256,256]{2,1,0:T(8,128)(2,1)S(1)}, bf16[8,256,256]{2,1,0:T(8,128)(2,1)}, u32[]{:S(2)}) copy-start(bf16[8,256,256]{2,1,0:T(8,128)(2,1)} %prefix_ref.1) | copy-start | bytes 3145732
  41.5 18.3 %copy-start = (bf16[64,1,16,256]{3,2,1,0:T(8,128)(2,1)S(1)}, bf16[64,1,16,256]{3,2,1,0:T(8,128)(2,1)}, u32[]{:S(2)}) copy-start(bf16[64,1,16,256]{3,2,1,0:T(8,128)(2,1)} %param.14) | copy-start | bytes 1572868
  41.6 18.2 %copy-start.2 = (f32[10,16,128]{2,1,0:T(8,128)S(1)}, f32[10,16,128]{2,1,0:T(8,128)}, u32[]{:S(2)}) copy-start(f32[10,16,128]{2,1,0:T(8,128)} %get-tuple-element.10.seen_ref) | copy-start | bytes 245764
  83.2 29.1 %copy-start.3 = (bf16[1024,128]{1,0:T(8,128)(2,1)S(1)}, bf16[1024,128]{1,0:T(8,128)(2,1)}, u32[]{:S(2)}) copy-start(bf16[1024,128]{1,0:T(8,128)(2,1)} %weight_ref.1) | copy-start | bytes 786436

commit v3 on v2

--- a/solution.py
+++ b/solution.py
@@ -19,8 +19,12 @@
 MIB = 1024 * 1024
 F32, BF16 = jnp.float32, jnp.bfloat16
 
-KEYS_AT, VALUES_AT, FRESH_AT, SENT = ROWS, ROWS + PAGE, ROWS + 2 * PAGE, ROWS + 2 * PAGE + BW
-PACK = ROWS + 8
+LX, LY, LC = 4, 8, 2
+ALONG_XC = [[(x * LY + y) * LC + c for x in range(LX) for c in range(LC)] for y in range(LY)]
+ALONG_Y = [[(x * LY + y) * LC + c for y in range(LY)] for x in range(LX) for c in range(LC)]
+
+KEYS_AT, VALUES_AT, SHARE = GROUP * ROWS, (GROUP + 1) * ROWS, (GROUP + 2) * ROWS
+STATS_AT, PACK = ROWS + 2 * PAGE, ROWS + 2 * PAGE + 8
 CARRY = ROWS + 2 * PAGE
 
 VMEM = pl.BlockSpec(memory_space=pltpu.VMEM)
@@ -43,6 +47,15 @@
     return lax.broadcasted_iota(jnp.int32, shape, dim)
 
 
+def device_of(p, k):
+    return (p // LC * LY + k) * LC + p % LC
+
+
+def place():
+    me = lax.axis_index("ctx")
+    return me, (me >> 4) * LC + (me & 1), (me >> 1) & (LY - 1)
+
+
 def project_kernel(
     parents_ref,
     start_ref,
@@ -52,6 +65,7 @@
     table_hbm,
     pages_hbm,
     out_ref,
+    moved_ref,
     seen_ref,
     hidden_ref,
     weight_ref,
@@ -60,7 +74,7 @@
     pages_ref,
     sems,
 ):
-    me = lax.axis_index("ctx")
+    me, prompt, beam = place()
     pairs = (
         (hidden_hbm, hidden_ref),
         (weight_hbm, weight_ref),
@@ -89,7 +103,7 @@
         old_seen = (lane // PAGE == holder) & jnp.logical_not(stale)
         seen_ref[p] = jnp.where(old_seen, 0.0, -jnp.inf)
 
-    base = (me >> 3) * BW
+    base = prompt * BW
     first_new = jnp.zeros((ROWS, HD), jnp.int32)
     for b in range(BW):
         first_new = jnp.where(row == b, b, first_new)
@@ -97,9 +111,9 @@
     second_new = jnp.where(row < BW, first_new, row)
     seen_ref[prompts] = jnp.where((lane == first_new) | (lane == second_new), 0.0, -jnp.inf)
 
-    near = parents_ref[1, me]
-    shift = (start_ref[2, me] - start_ref[0, parents_ref[0, near]]) & (CTX - 1)
-    last = (start_ref[2, me] - 1) & (CTX - 1)
+    near = parents_ref[1, base + beam]
+    shift = (start_ref[2, base + beam] - start_ref[0, parents_ref[0, near]]) & (CTX - 1)
+    last = (start_ref[2, base + beam] - 1) & (CTX - 1)
     facts = jnp.where(row == 0, shift, jnp.where(row == 1, last, near - base))
     seen_ref[prompts + 1] = facts.astype(F32)
 
@@ -107,8 +121,9 @@
         copy.wait()
     for c in range(beams):
         far = parents_ref[0, parents_ref[1, c]]
-        out_ref[c, KEYS_AT:VALUES_AT, :] = pages_ref[far, :, :HD]
-        out_ref[c, VALUES_AT:FRESH_AT, :] = pages_ref[far, :, HD:]
+        to = device_of(c // BW, c % BW)
+        moved_ref[to, :PAGE, :] = pages_ref[far, :, :HD]
+        moved_ref[to, PAGE:, :] = pages_ref[far, :, HD:]
 
     cosine = [jnp.broadcast_to(table_ref[s : s + 1], (BW, HD)) for s in range(STEPS)]
     sine = [jnp.broadcast_to(table_ref[STEPS + s : STEPS + s + 1], (BW, HD)) for s in range(STEPS)]
@@ -125,29 +140,23 @@
         part = part + bias[col : col + 1]
         if col <= GROUP:
             part = part * cosine + pltpu.roll(part, HD // 2, 1) * sine
+        part = part.astype(BF16)
         for p in range(prompts):
-            tile = part[p * ROWS : (p + 1) * ROWS]
-            if col < GROUP:
-                out_ref[p * GROUP + col, :ROWS, :] = tile.astype(BF16)
-            else:
-                for h in range(GROUP):
-                    if h % 2 == col - GROUP:
-                        s = h // 2 % 2
-                        out_ref[p * GROUP + h, FRESH_AT:, :] = tile[s * BW : (s + 1) * BW].astype(
-                            BF16
-                        )
+            out_ref[p, col * ROWS : (col + 1) * ROWS, :] = part[p * ROWS : (p + 1) * ROWS]
+
+
+def row_sum_kernel(parts_ref, out_ref):
+    total = jnp.sum(parts_ref[...].astype(F32), axis=0).astype(BF16)
+    out_ref[...] = jnp.broadcast_to(total[None], out_ref.shape)
 
 
 def sum_kernel(parts_ref, out_ref, own_ref):
-    query = jnp.sum(parts_ref[:, :ROWS, :].astype(F32), axis=0).astype(BF16)
-    fresh = jnp.sum(parts_ref[:, FRESH_AT:, :].astype(F32), axis=0).astype(BF16)
-    out_ref[...] = jnp.broadcast_to(query[None], out_ref.shape)
-    own_ref[:ROWS, :] = query
-    own_ref[ROWS:, :] = fresh
-
-
-def attend_kernel(shared_ref, prefix_ref, pages_ref, seen_ref, own_ref, out_ref):
-    h_me = lax.axis_index("ctx") & (GROUP - 1)
+    total = jnp.sum(parts_ref[...].astype(F32), axis=0).astype(BF16)
+    out_ref[...] = jnp.broadcast_to(total[None, :KEYS_AT], out_ref.shape)
+    own_ref[...] = total
+
+
+def attend_kernel(shared_ref, prefix_ref, pages_ref, seen_ref, moved_ref, out_ref):
     prompts = prefix_ref.shape[0]
     scale = HD**-0.5
     contract = (((1,), (1,)), ((), ()))
@@ -155,11 +164,7 @@
     row = iota((GROUP * ROWS, HD), 0)
     slot = lane // ROWS
     diagonal = lane % ROWS == row % ROWS
-
-    fresh = own_ref[ROWS:, :].astype(F32)
-    fresh = jnp.where(h_me < GROUP // 2, pltpu.roll(fresh, 4, 0), fresh)
     line = iota((8, HD), 0)
-    fresh = jnp.where(line >= 4, fresh, 0.0)
 
     def split(value):
         high = value.astype(BF16).astype(F32)
@@ -168,7 +173,7 @@
         return high, mid, rest - mid
 
     for p in range(prompts):
-        query = shared_ref[p * GROUP : (p + 1) * GROUP].reshape(GROUP * ROWS, HD)
+        query = shared_ref[p]
         tail = pages_ref[p * BW : (p + 1) * BW].reshape(BW * PAGE, 2 * HD)
         s_pre = (
             lax.dot_general(query, prefix_ref[p, :, :HD], contract, preferred_element_type=F32)
@@ -186,46 +191,33 @@
         mixed = jnp.dot(
             w_pre.astype(BF16), prefix_ref[p, :, HD:], preferred_element_type=F32
         ) + jnp.dot(w_old.astype(BF16), tail[:, HD:], preferred_element_type=F32)
-        out_ref[p * GROUP : (p + 1) * GROUP, :ROWS, :] = mixed.astype(BF16).reshape(
-            GROUP, ROWS, HD
-        )
+        mixed = mixed.astype(BF16)
         table = jnp.zeros((GROUP * ROWS, HD), F32)
         for k, term in enumerate(split(peak) + split(total)):
             table = jnp.where(slot == k, term, table)
         table = jnp.sum(jnp.where(diagonal, table, 0.0).reshape(GROUP, ROWS, HD), axis=1)
         for h in range(GROUP):
-            out_ref[p * GROUP + h, ROWS:, :] = jnp.where(
-                line == 0, table[h : h + 1], fresh
-            ).astype(BF16)
-
-
-def merge_kernel(parts_ref, own_ref, seen_ref, first_ref, out_ref):
-    me = lax.axis_index("ctx")
-    base = (me >> 3) * GROUP
+            to = device_of(p, h)
+            out_ref[to, :ROWS, :] = mixed[h * ROWS : (h + 1) * ROWS]
+            out_ref[to, ROWS:STATS_AT, :] = moved_ref[to]
+            out_ref[to, STATS_AT:, :] = jnp.where(line == 0, table[h : h + 1], 0.0).astype(BF16)
+
+
+def merge_kernel(parts_ref, own_ref, seen_ref, out_ref):
+    _, _, beam = place()
     prompts = seen_ref.shape[0] - 2
-    line = iota((8, HD), 0)
-
-    def gather(kv):
-        tiles = []
-        for s in range(STEPS):
-            low = parts_ref[base + 2 * s + kv, ROWS:, :].astype(F32)
-            high = parts_ref[base + 2 * s + kv + GROUP // 2, ROWS:, :].astype(F32)
-            tiles.append(jnp.where(line < 4, pltpu.roll(low, 4, 0), high))
-        return tiles
-
-    new_keys, new_values = gather(0), gather(1)
-    blank = [jnp.zeros((HD - ROWS, HD), F32)]
-    key = jnp.concatenate(new_keys + blank, axis=0).astype(BF16)
-    value = jnp.concatenate(new_values + blank, axis=0).astype(BF16)
+
+    blank = jnp.zeros((HD - ROWS, HD), BF16)
+    key = jnp.concatenate([own_ref[KEYS_AT:VALUES_AT, :], blank], axis=0)
+    value = jnp.concatenate([own_ref[VALUES_AT:, :], blank], axis=0)
+    query = own_ref[pl.ds(pl.multiple_of(beam * ROWS, ROWS), ROWS), :]
     s_new = (
-        lax.dot_general(
-            own_ref[:ROWS, :], key, (((1,), (1,)), ((), ())), preferred_element_type=F32
-        )
+        lax.dot_general(query, key, (((1,), (1,)), ((), ())), preferred_element_type=F32)
         * HD**-0.5
         + seen_ref[prompts]
     )
 
-    stats = parts_ref[:, ROWS:, :].astype(F32)
+    stats = parts_ref[:, STATS_AT:, :].astype(F32)
     stats = jnp.sum(jnp.where(iota(stats.shape, 1) == 0, stats, 0.0), axis=1)
 
     def term(k):
@@ -253,14 +245,15 @@
     last = jnp.max(facts[1:2]).astype(jnp.int32)
     for k in range(CTX):
         out_ref[k, :ROWS, :] = attention
-        out_ref[k, ROWS:, :] = first_ref[(k - shift) & (CTX - 1), KEYS_AT:FRESH_AT, :]
-
-    mine = (me & (BW - 1)).astype(F32)
-    place = line.astype(F32)
+        out_ref[k, ROWS:, :] = parts_ref[(k - shift) & (CTX - 1), ROWS:STATS_AT, :]
+
     row = iota((PAGE, HD), 0)
-    for at, tiles in ((ROWS, new_keys), (ROWS + PAGE, new_values)):
-        earlier = jnp.sum(jnp.where(place == facts[2:3], tiles[0], 0.0), axis=0, keepdims=True)
-        newest = jnp.sum(jnp.where(place == mine, tiles[1], 0.0), axis=0, keepdims=True)
+    line = row.astype(F32)
+    mine = (BW + beam).astype(F32)
+    for at, rows in ((ROWS, key), (ROWS + PAGE, value)):
+        rows = rows[:ROWS].astype(F32)
+        earlier = jnp.sum(jnp.where(line == facts[2:3], rows, 0.0), axis=0, keepdims=True)
+        newest = jnp.sum(jnp.where(line == mine, rows, 0.0), axis=0, keepdims=True)
         page = out_ref[last, at : at + PAGE, :].astype(F32)
         page = jnp.where(row == PAGE - 2, earlier, page)
         page = jnp.where(row == PAGE - 1, newest, page)
@@ -271,7 +264,8 @@
     prompts = out_ref.shape[0]
     acc = jnp.zeros((prompts * ROWS, HD), F32)
     for h in range(GROUP):
-        head = jnp.concatenate([heads_ref[p * GROUP + h, :ROWS, :] for p in range(prompts)], axis=0)
+        head = [heads_ref[device_of(p, h), :ROWS, :] for p in range(prompts)]
+        head = jnp.concatenate(head, axis=0)
         acc = acc + jnp.dot(
             head, weight_ref[h * HD : (h + 1) * HD, :], preferred_element_type=F32
         )
@@ -279,14 +273,16 @@
 
 
 def finish_kernel(share_ref, heads_hbm, out_ref, tail_hbm, sems):
-    copies = [
-        pltpu.make_async_copy(
-            heads_hbm.at[:, pl.ds(ROWS + k * PAGE, PAGE), :],
-            tail_hbm.at[:, :, pl.ds(k * HD, HD)],
-            sems.at[k],
-        )
-        for k in range(2)
-    ]
+    copies = []
+    for core in range(LC):
+        for k in range(2):
+            copies.append(
+                pltpu.make_async_copy(
+                    heads_hbm.at[:, :, core, pl.ds(ROWS + k * PAGE, PAGE), :],
+                    tail_hbm.at[:, core, :, :, pl.ds(k * HD, HD)],
+                    sems.at[2 * core + k],
+                )
+            )
     for copy in copies:
         copy.start()
     total = jnp.sum(share_ref[...].astype(F32), axis=0)
@@ -316,11 +312,17 @@
     pages = tail_cache.reshape(beams, PAGE, 2 * HD)
     bias = qkv_bias.reshape(GROUP + 2, HD)
     table = rope_rows()
-    swap = functools.partial(lax.all_to_all, split_axis=0, concat_axis=0, tiled=True)
-
-    parts, seen = call(
+    swap = functools.partial(
+        lax.all_to_all, axis_name="ctx", split_axis=0, concat_axis=0, tiled=True
+    )
+
+    parts, moved, seen = call(
         project_kernel,
-        [((CTX, SENT, HD), BF16), ((prompts + 2, ROWS, HD), F32)],
+        [
+            ((prompts, SHARE, HD), BF16),
+            ((CTX, 2 * PAGE, HD), BF16),
+            ((prompts + 2, ROWS, HD), F32),
+        ],
         [SMEM] * 2 + [HBM] * 5,
         [
             pltpu.VMEM(hidden.shape, BF16),
@@ -332,28 +334,28 @@
         ],
         limit=60,
     )(parents, start_dev, hidden, qkv_weight, bias, table, pages)
-    first = swap(parts, "ctx")
+    parts = swap(parts, axis_index_groups=ALONG_XC)
+    (parts,) = call(row_sum_kernel, [((LY, SHARE, HD), BF16)], [VMEM])(parts)
+    parts = swap(parts, axis_index_groups=ALONG_Y)
     mine, own = call(
-        sum_kernel, [((CTX, ROWS, HD), BF16), ((ROWS + BW, HD), BF16)], [VMEM]
-    )(first)
-    shared = swap(mine, "ctx")
+        sum_kernel, [((prompts, KEYS_AT, HD), BF16), ((SHARE, HD), BF16)], [VMEM]
+    )(parts)
+    shared = swap(mine, axis_index_groups=ALONG_XC)
     (parts,) = call(attend_kernel, [((CTX, PACK, HD), BF16)], [VMEM] * 5)(
-        shared, prefix_cache, pages, seen, own
-    )
-    parts = swap(parts, "ctx")
-    (merged,) = call(merge_kernel, [((CTX, CARRY, HD), BF16)], [VMEM] * 4)(
-        parts, own, seen, first
-    )
-    heads = swap(merged, "ctx")
+        shared, prefix_cache, pages, seen, moved
+    )
+    parts = swap(parts)
+    (merged,) = call(merge_kernel, [((CTX, CARRY, HD), BF16)], [VMEM] * 3)(parts, own, seen)
+    heads = swap(merged)
     (share,) = call(output_kernel, [((prompts, ROWS, HD), BF16)], [VMEM] * 2)(heads, out_weight)
-    share = swap(share, "tp")
+    share = swap(share, axis_name="tp")
     attended, tail_out = call(
         finish_kernel,
-        [((STEPS, BW, HD), BF16), ((beams, PAGE, 2 * HD), BF16)],
+        [((STEPS, BW, HD), BF16), ((LX, LC, LY, PAGE, 2 * HD), BF16)],
         [VMEM, HBM],
-        [pltpu.SemaphoreType.DMA((2,))],
+        [pltpu.SemaphoreType.DMA((4,))],
         out_specs=[VMEM, HBM],
-    )(share, heads)
+    )(share, heads.reshape(LX, LY, LC, CARRY, HD))
     return attended, tail_out.reshape(tail_cache.shape)
 
 

time: 131 us -> 129 us (0.985)
  blocking collectives: 122 us -> 120 us
    all_to_all x5 -> x6, blocking collectives: 122 us -> 120 us  [the longest x1 30.1 us: per_device(): parts = swap(parts)]
    pallas_call x4 -> x5, Pallas kernels: 5.5 us -> 5.43 us  [the longest x1 3.26 us: per_device(): call(project_kernel, [((prompts, SHARE, HD), BF16), ((CTX, 2 * PAGE, HD),...]
where the time goes in v3:
time: 129 us; the launch traced here: 128 us
  blocking collectives  120 us (93%)
  Pallas kernels  7.97 us (6%)
    all_to_all x1, blocking collectives, per_device(): parts = swap(parts)  30.1 us
    all_to_all x1, blocking collectives, per_device(): heads = swap(merged)  29.2 us
    all_to_all x1, blocking collectives, per_device(): parts = swap(parts, axis_index_groups=ALONG_XC)  17.9 us
    all_to_all x1, blocking collectives, per_device(): share = swap(share, axis_name='tp')  16.6 us
    all_to_all x1, blocking collectives, per_device(): parts = swap(parts, axis_index_groups=ALONG_Y)  14.9 us
    all_to_all x1, blocking collectives, per_device(): shared = swap(mine, axis_index_groups=ALONG_XC)  10.9 us
    pallas_call x1, Pallas kernels, per_device(): call(project_kernel, [((prompts, SHARE, HD), BF16), ((CTX, 2 * PAGE, HD),...  3.26 us

profile of v3, /device:TPU:1, one launch (start us, length us, event | category | flops | bytes accessed | tf_op | source)
XLA Modules:
  0.0 128.3 jit_solution(469666394541887358)
XLA Ops:
  0.6 3.3 %shard_map.104 = (bf16[8,160,128]{2,1,0:T(8,128)(2,1)}, bf16[64,32,128]{2,1,0:T(8,128)(2,1)}, f32[10,16,128]{2,1,0:T(8,128)}) custom-call(s32[2,64]{1,0:T(2,128)} %parents_ref.1, s32[3,64]{1,0:T(4,128)} %start_ref.1, bf16[2,64,128]{2,1,0:T(8,128)(2,1)} %hidden_hbm.1, bf16[128,1280]{1,0:T(8,128)(2,1)} %weight_hbm.1, bf16[10,128]{1,0:T(8,128)(2,1)} %bitcast.9, ...), custom_call_target="tpu_custom_call" | custom-call | tf_op jit(solution)/shard_map/pallas_call | solution.py:319
  3.9 0.0 copy-start.3
  3.9 17.9 %all_to_all.30.parts_ref = bf16[8,160,128]{2,1,0:T(8,128)(2,1)S(1)} all-to-all(bf16[8,160,128]{2,1,0:T(8,128)(2,1)} %get-tuple-element.9), channel_id=1, replica_groups={{0,8,128,136,256,264,384,392},{16,24,144,152,272,280,400,408},{32,40,16..., dimensions={0} | all-to-all | bytes 655360 | tf_op jit(solution)/shard_map/all_to_all | solution.py:337
  21.8 0.0 copy-start.1
  21.8 0.0 copy-start.2
  21.8 14.9 %all_to_all.31.parts_ref = bf16[8,160,128]{2,1,0:T(8,128)(2,1)S(1)} all-to-all(bf16[8,160,128]{2,1,0:T(8,128)(2,1)S(1)} %shard_map.105), channel_id=1, replica_groups={{0,16,32,48,64,80,96,112},{8,24,40,56,72,88,104,120},{128,144,160,176,1..., dimensions={0} | all-to-all | bytes 655360 | tf_op jit(solution)/shard_map/all_to_all | solution.py:339
  36.7 0.0 copy-start
  36.7 10.9 %all_to_all.32.shared_ref = bf16[8,128,128]{2,1,0:T(8,128)(2,1)S(1)} all-to-all(bf16[8,128,128]{2,1,0:T(8,128)(2,1)S(1)} %get-tuple-element.10), channel_id=1, replica_groups={{0,8,128,136,256,264,384,392},{16,24,144,152,272,280,400,408},{32,40,16..., dimensions={0} | all-to-all | bytes 524288 | tf_op jit(solution)/shard_map/all_to_all | solution.py:343
  47.7 0.0 copy-done.3
  47.7 0.0 copy-done.1
  47.7 0.0 copy-done.2
  47.7 0.0 copy-done
  47.7 2.3 %shard_map.107 = bf16[64,56,128]{2,1,0:T(8,128)(2,1)S(1)} custom-call(bf16[8,128,128]{2,1,0:T(8,128)(2,1)S(1)} %all_to_all.32.shared_ref, bf16[8,256,256]{2,1,0:T(8,128)(2,1)S(1)} %copy-done.1, bf16[64,16,256]{2,1,0:T(8,128)(2,1)S(1)} %bitcast.8, f32[10,16,128]{2,1,0:T(8,128)S(1)} %copy-done.3, bf16[64,32,128]{2,1,0:T(8,128)(2,1)S(1)} %copy-done.2), custom_call_target="tpu_custom_call" | custom-call | tf_op jit(solution)/shard_map/pallas_call | solution.py:344
  50.0 30.1 %all_to_all.33.parts_ref = bf16[64,56,128]{2,1,0:T(8,128)(2,1)S(1)} all-to-all(bf16[64,56,128]{2,1,0:T(8,128)(2,1)S(1)} %shard_map.107), channel_id=1, replica_groups=mesh['ctx'=64,'tp'=8] {'ctx'}, dimensions={0} | all-to-all | bytes 1835008 | tf_op jit(solution)/shard_map/all_to_all | solution.py:347
  80.1 0.7 shard_map.108
  80.8 0.0 copy-start.4
  80.8 29.2 %all_to_all.34.heads_ref = bf16[64,48,128]{2,1,0:T(8,128)(2,1)S(1)} all-to-all(bf16[64,48,128]{2,1,0:T(8,128)(2,1)S(1)} %shard_map.108), channel_id=1, replica_groups=mesh['ctx'=64,'tp'=8] {'ctx'}, dimensions={0} | all-to-all | bytes 1572864 | tf_op jit(solution)/shard_map/all_to_all | solution.py:349
  110.0 0.0 copy-done.4
  110.0 0.2 shard_map.109
  110.2 16.6 %all_to_all.35.share_ref = bf16[8,16,128]{2,1,0:T(8,128)(2,1)S(1)} all-to-all(bf16[8,16,128]{2,1,0:T(8,128)(2,1)S(1)} %shard_map.109), channel_id=1, replica_groups=mesh['ctx'=64,'tp'=8] {'tp'}, dimensions={0} | all-to-all | bytes 65536 | tf_op jit(solution)/shard_map/all_to_all | solution.py:351
  126.8 1.4 %shard_map.110 = (bf16[2,8,128]{2,1,0:T(8,128)(2,1)}, bf16[4,2,8,16,256]{4,3,2,1,0:T(8,128)(2,1)}) custom-call(bf16[8,16,128]{2,1,0:T(8,128)(2,1)S(1)} %all_to_all.35.share_ref, bf16[4,8,2,48,128]{4,3,2,1,0:T(8,128)(2,1)S(1)} %bitcast.6), custom_call_target="tpu_custom_call" | custom-call | tf_op jit(solution)/shard_map/pallas_call | solution.py:352
  (2 shorter events, 0.1 us)
Async XLA Ops:
  3.9 43.8 %copy-start.3 = (f32[10,16,128]{2,1,0:T(8,128)S(1)}, f32[10,16,128]{2,1,0:T(8,128)}, u32[]{:S(2)}) copy-start(f32[10,16,128]{2,1,0:T(8,128)} %get-tuple-element.11.seen_ref) | copy-start | bytes 245764
  21.8 25.9 %copy-start.1 = (bf16[8,256,256]{2,1,0:T(8,128)(2,1)S(1)}, bf16[8,256,256]{2,1,0:T(8,128)(2,1)}, u32[]{:S(2)}) copy-start(bf16[8,256,256]{2,1,0:T(8,128)(2,1)} %prefix_ref.1) | copy-start | bytes 3145732
  21.8 25.9 %copy-start.2 = (bf16[64,32,128]{2,1,0:T(8,128)(2,1)S(1)}, bf16[64,32,128]{2,1,0:T(8,128)(2,1)}, u32[]{:S(2)}) copy-start(bf16[64,32,128]{2,1,0:T(8,128)(2,1)} %get-tuple-element.12.moved_ref) | copy-start | bytes 1572868
  36.7 11.0 %copy-start = (bf16[64,1,16,256]{3,2,1,0:T(8,128)(2,1)S(1)}, bf16[64,1,16,256]{3,2,1,0:T(8,128)(2,1)}, u32[]{:S(2)}) copy-start(bf16[64,1,16,256]{3,2,1,0:T(8,128)(2,1)} %param.14) | copy-start | bytes 1572868
  80.8 29.2 %copy-start.4 = (bf16[1024,128]{1,0:T(8,128)(2,1)S(1)}, bf16[1024,128]{1,0:T(8,128)(2,1)}, u32[]{:S(2)}) copy-start(bf16[1024,128]{1,0:T(8,128)(2,1)} %weight_ref.1) | copy-start | bytes 786436

commit v4 on v3

--- a/solution.py
+++ b/solution.py
@@ -24,7 +24,7 @@
 ALONG_Y = [[(x * LY + y) * LC + c for y in range(LY)] for x in range(LX) for c in range(LC)]
 
 KEYS_AT, VALUES_AT, SHARE = GROUP * ROWS, (GROUP + 1) * ROWS, (GROUP + 2) * ROWS
-STATS_AT, PACK = ROWS + 2 * PAGE, ROWS + 2 * PAGE + 8
+STATS_AT, PACK = ROWS + LX * LC * 2 * PAGE, ROWS + LX * LC * 2 * PAGE + 8
 CARRY = ROWS + 2 * PAGE
 
 VMEM = pl.BlockSpec(memory_space=pltpu.VMEM)
@@ -63,68 +63,81 @@
     weight_hbm,
     bias_hbm,
     table_hbm,
+    prefix_hbm,
     pages_hbm,
     out_ref,
-    moved_ref,
     seen_ref,
+    pick_ref,
     hidden_ref,
     weight_ref,
     bias_ref,
     table_ref,
-    pages_ref,
     sems,
 ):
-    me, prompt, beam = place()
-    pairs = (
+    pairs = [
         (hidden_hbm, hidden_ref),
         (weight_hbm, weight_ref),
         (bias_hbm, bias_ref),
         (table_hbm, table_ref),
-        (pages_hbm, pages_ref),
-    )
+    ]
+    needed = len(pairs)
+    prompts, tokens = prefix_hbm.shape[:2]
+    tail = BW * PAGE
+    for p in range(prompts):
+        at = SHARE
+        for source, count in (
+            (prefix_hbm.at[p], tokens),
+            (pages_hbm.at[pl.ds(p * tail, tail)], tail),
+        ):
+            for k in range(2):
+                lanes = source.at[:, pl.ds(k * HD, HD)]
+                pairs.append((lanes, out_ref.at[p, pl.ds(at, count), :]))
+                at += count
     copies = [pltpu.make_async_copy(a, b, sems.at[k]) for k, (a, b) in enumerate(pairs)]
     for copy in copies:
         copy.start()
-    prompts = hidden_ref.shape[1] // BW
-    beams = prompts * BW
+
+    _, prompt, beam = place()
+    base = prompt * BW
     lane = iota((ROWS, HD), 1)
     row = iota((ROWS, HD), 0)
-
-    for p in range(prompts):
-        holder = jnp.zeros((ROWS, HD), jnp.int32)
-        stale = lane < 0
-        for b in range(BW):
-            near = parents_ref[1, p * BW + b]
-            holder = jnp.where(row == b, parents_ref[0, p * BW + b] - p * BW, holder)
-            holder = jnp.where(row == BW + b, parents_ref[0, near] - p * BW, holder)
-            last_page = ((me - start_ref[0, p * BW + b]) & (CTX - 1)) == CTX - 1
-            cut = jnp.where(last_page, PAGE - STEPS, PAGE)
-            stale = stale | ((lane // PAGE == b) & (lane % PAGE >= cut))
+    holder = jnp.zeros((ROWS, HD), jnp.int32)
+    first = jnp.zeros((ROWS, HD), jnp.int32)
+    for b in range(BW):
+        near = parents_ref[1, base + b]
+        holder = jnp.where(row == b, parents_ref[0, base + b] - base, holder)
+        holder = jnp.where(row == BW + b, parents_ref[0, near] - base, holder)
+        first = jnp.where(lane // PAGE == b, start_ref[0, base + b], first)
+    for u in range(LX * LC):
+        device = (u // LC * LY + beam) * LC + u % LC
+        last_page = ((device - first) & (CTX - 1)) == CTX - 1
+        stale = last_page & (lane % PAGE >= PAGE - STEPS)
         old_seen = (lane // PAGE == holder) & jnp.logical_not(stale)
-        seen_ref[p] = jnp.where(old_seen, 0.0, -jnp.inf)
-
-    base = prompt * BW
+        seen_ref[u] = jnp.where(old_seen, 0.0, -jnp.inf)
+
     first_new = jnp.zeros((ROWS, HD), jnp.int32)
     for b in range(BW):
         first_new = jnp.where(row == b, b, first_new)
         first_new = jnp.where(row == BW + b, parents_ref[1, base + b] - base, first_new)
     second_new = jnp.where(row < BW, first_new, row)
-    seen_ref[prompts] = jnp.where((lane == first_new) | (lane == second_new), 0.0, -jnp.inf)
+    seen_ref[LX * LC] = jnp.where((lane == first_new) | (lane == second_new), 0.0, -jnp.inf)
 
     near = parents_ref[1, base + beam]
     shift = (start_ref[2, base + beam] - start_ref[0, parents_ref[0, near]]) & (CTX - 1)
     last = (start_ref[2, base + beam] - 1) & (CTX - 1)
     facts = jnp.where(row == 0, shift, jnp.where(row == 1, last, near - base))
-    seen_ref[prompts + 1] = facts.astype(F32)
-
-    for copy in copies:
+    seen_ref[LX * LC + 1] = facts.astype(F32)
+
+    lane = iota((tail, HD), 1)
+    row = iota((tail, HD), 0)
+    wanted = jnp.zeros((tail, HD), jnp.int32)
+    for b in range(BW):
+        far = parents_ref[0, parents_ref[1, base + b]] - base
+        wanted = jnp.where(row // PAGE == b, far * PAGE + row % PAGE, wanted)
+    pick_ref[...] = jnp.where(lane == wanted, 1.0, 0.0).astype(BF16)
+
+    for copy in copies[:needed]:
         copy.wait()
-    for c in range(beams):
-        far = parents_ref[0, parents_ref[1, c]]
-        to = device_of(c // BW, c % BW)
-        moved_ref[to, :PAGE, :] = pages_ref[far, :, :HD]
-        moved_ref[to, PAGE:, :] = pages_ref[far, :, HD:]
-
     cosine = [jnp.broadcast_to(table_ref[s : s + 1], (BW, HD)) for s in range(STEPS)]
     sine = [jnp.broadcast_to(table_ref[STEPS + s : STEPS + s + 1], (BW, HD)) for s in range(STEPS)]
     cosine = jnp.concatenate(cosine * prompts, axis=0)
@@ -143,21 +156,21 @@
         part = part.astype(BF16)
         for p in range(prompts):
             out_ref[p, col * ROWS : (col + 1) * ROWS, :] = part[p * ROWS : (p + 1) * ROWS]
+    for copy in copies[needed:]:
+        copy.wait()
 
 
 def row_sum_kernel(parts_ref, out_ref):
-    total = jnp.sum(parts_ref[...].astype(F32), axis=0).astype(BF16)
+    total = jnp.sum(parts_ref[:, :SHARE, :].astype(F32), axis=0).astype(BF16)
     out_ref[...] = jnp.broadcast_to(total[None], out_ref.shape)
 
 
-def sum_kernel(parts_ref, out_ref, own_ref):
-    total = jnp.sum(parts_ref[...].astype(F32), axis=0).astype(BF16)
-    out_ref[...] = jnp.broadcast_to(total[None, :KEYS_AT], out_ref.shape)
-    own_ref[...] = total
-
-
-def attend_kernel(shared_ref, prefix_ref, pages_ref, seen_ref, moved_ref, out_ref):
-    prompts = prefix_ref.shape[0]
+def attend_kernel(sums_ref, cache_ref, seen_ref, pick_ref, out_ref, own_ref, score_ref):
+    chunks = cache_ref.shape[0]
+    tail = BW * PAGE
+    tokens = (cache_ref.shape[1] - SHARE) // 2 - tail
+    v_at, tk_at = SHARE + tokens, SHARE + 2 * tokens
+    tv_at = tk_at + tail
     scale = HD**-0.5
     contract = (((1,), (1,)), ((), ()))
     lane = iota((GROUP * ROWS, HD), 1)
@@ -172,40 +185,58 @@
         mid = rest.astype(BF16).astype(F32)
         return high, mid, rest - mid
 
-    for p in range(prompts):
-        query = shared_ref[p]
-        tail = pages_ref[p * BW : (p + 1) * BW].reshape(BW * PAGE, 2 * HD)
-        s_pre = (
-            lax.dot_general(query, prefix_ref[p, :, :HD], contract, preferred_element_type=F32)
-            * scale
+    total = jnp.sum(sums_ref[...].astype(F32), axis=0).astype(BF16)
+    own_ref[...] = total
+    query = total[:KEYS_AT]
+    peak = jnp.full((GROUP * ROWS, HD), -jnp.inf, F32)
+    for u in range(chunks):
+        keys = cache_ref[u, SHARE:v_at, :]
+        score = lax.dot_general(query, keys, contract, preferred_element_type=F32) * scale
+        score_ref[u, :, :tokens] = score
+        for k in range(0, tokens, HD):
+            peak = jnp.maximum(peak, score[:, k : k + HD])
+        keys = cache_ref[u, tk_at:tv_at, :]
+        score = lax.dot_general(query, keys, contract, preferred_element_type=F32) * scale
+        score = score + jnp.concatenate([seen_ref[u]] * GROUP, axis=0)
+        score_ref[u, :, tokens:] = score
+        peak = jnp.maximum(peak, score)
+    peak = jnp.max(peak, axis=1, keepdims=True)
+    total = jnp.zeros((GROUP * ROWS, HD), F32)
+    mixed = jnp.zeros((GROUP * ROWS, HD), F32)
+    for u in range(chunks):
+        weight = jnp.exp(score_ref[u] - peak)
+        for k in range(0, tokens + tail, HD):
+            total = total + weight[:, k : k + HD]
+        weight = weight.astype(BF16)
+        mixed = mixed + jnp.dot(
+            weight[:, :tokens], cache_ref[u, v_at:tk_at, :], preferred_element_type=F32
         )
-        s_old = lax.dot_general(
-            query, tail[:, :HD], contract, preferred_element_type=F32
-        ) * scale + jnp.concatenate([seen_ref[p]] * GROUP, axis=0)
-        peak = jnp.maximum(
-            jnp.max(s_pre, axis=1, keepdims=True), jnp.max(s_old, axis=1, keepdims=True)
+        mixed = mixed + jnp.dot(
+            weight[:, tokens:], cache_ref[u, tv_at:, :], preferred_element_type=F32
         )
-        w_pre = jnp.exp(s_pre - peak)
-        w_old = jnp.exp(s_old - peak)
-        total = jnp.sum(w_pre, axis=1, keepdims=True) + jnp.sum(w_old, axis=1, keepdims=True)
-        mixed = jnp.dot(
-            w_pre.astype(BF16), prefix_ref[p, :, HD:], preferred_element_type=F32
-        ) + jnp.dot(w_old.astype(BF16), tail[:, HD:], preferred_element_type=F32)
-        mixed = mixed.astype(BF16)
-        table = jnp.zeros((GROUP * ROWS, HD), F32)
-        for k, term in enumerate(split(peak) + split(total)):
-            table = jnp.where(slot == k, term, table)
-        table = jnp.sum(jnp.where(diagonal, table, 0.0).reshape(GROUP, ROWS, HD), axis=1)
-        for h in range(GROUP):
-            to = device_of(p, h)
-            out_ref[to, :ROWS, :] = mixed[h * ROWS : (h + 1) * ROWS]
-            out_ref[to, ROWS:STATS_AT, :] = moved_ref[to]
-            out_ref[to, STATS_AT:, :] = jnp.where(line == 0, table[h : h + 1], 0.0).astype(BF16)
+    total = jnp.sum(total, axis=1, keepdims=True)
+    mixed = mixed.astype(BF16)
+
+    table = jnp.zeros((GROUP * ROWS, HD), F32)
+    for k, term in enumerate(split(peak) + split(total)):
+        table = jnp.where(slot == k, term, table)
+    table = jnp.sum(jnp.where(diagonal, table, 0.0).reshape(GROUP, ROWS, HD), axis=1)
+    for h in range(GROUP):
+        out_ref[h, :ROWS, :] = mixed[h * ROWS : (h + 1) * ROWS]
+        out_ref[h, STATS_AT:, :] = jnp.where(line == 0, table[h : h + 1], 0.0).astype(BF16)
+
+    for u in range(chunks):
+        for k, at in enumerate((tk_at, tv_at)):
+            moved = jnp.dot(pick_ref[...], cache_ref[u, at : at + tail, :], preferred_element_type=F32)
+            moved = moved.astype(BF16)
+            for b in range(BW):
+                to = ROWS + (2 * u + k) * PAGE
+                out_ref[b, to : to + PAGE, :] = moved[b * PAGE : (b + 1) * PAGE]
 
 
 def merge_kernel(parts_ref, own_ref, seen_ref, out_ref):
     _, _, beam = place()
-    prompts = seen_ref.shape[0] - 2
+    masks = seen_ref.shape[0] - 2
 
     blank = jnp.zeros((HD - ROWS, HD), BF16)
     key = jnp.concatenate([own_ref[KEYS_AT:VALUES_AT, :], blank], axis=0)
@@ -214,7 +245,7 @@
     s_new = (
         lax.dot_general(query, key, (((1,), (1,)), ((), ())), preferred_element_type=F32)
         * HD**-0.5
-        + seen_ref[prompts]
+        + seen_ref[masks]
     )
 
     stats = parts_ref[:, STATS_AT:, :].astype(F32)
@@ -224,11 +255,11 @@
         return stats if k == 0 else pltpu.roll(stats, HD - k * ROWS, 1)
 
     def upright(table):
-        return jnp.concatenate([table, jnp.zeros((HD - CTX, HD), F32)], axis=0).T[:ROWS]
+        return jnp.concatenate([table, jnp.zeros((HD - LY, HD), F32)], axis=0).T[:ROWS]
 
     peak = upright(term(0) + term(1) + term(2))
     total = upright(term(3) + term(4) + term(5))
-    peak = jnp.where(iota((ROWS, HD), 1) < CTX, peak, -jnp.inf)
+    peak = jnp.where(iota((ROWS, HD), 1) < LY, peak, -jnp.inf)
     top = jnp.maximum(
         jnp.max(peak, axis=1, keepdims=True), jnp.max(s_new, axis=1, keepdims=True)
     )
@@ -236,16 +267,19 @@
     w_new = jnp.exp(s_new - top)
     denominator = jnp.sum(total * factor + w_new, axis=1, keepdims=True)
     acc = jnp.dot(w_new.astype(BF16), value, preferred_element_type=F32)
-    for k in range(CTX):
+    for k in range(LY):
         acc = acc + factor[:, k : k + 1] * parts_ref[k, :ROWS, :].astype(F32)
     attention = (acc / denominator).astype(BF16)
 
-    facts = seen_ref[prompts + 1]
+    facts = seen_ref[masks + 1]
     shift = jnp.max(facts[0:1]).astype(jnp.int32)
     last = jnp.max(facts[1:2]).astype(jnp.int32)
     for k in range(CTX):
         out_ref[k, :ROWS, :] = attention
-        out_ref[k, ROWS:, :] = parts_ref[(k - shift) & (CTX - 1), ROWS:STATS_AT, :]
+        held = (k - shift) & (CTX - 1)
+        column = (held >> 4) * LC + (held & 1)
+        at = pl.multiple_of(ROWS + column * 2 * PAGE, PAGE)
+        out_ref[k, ROWS:, :] = parts_ref[(held >> 1) & (LY - 1), pl.ds(at, 2 * PAGE), :]
 
     row = iota((PAGE, HD), 0)
     line = row.astype(F32)
@@ -309,42 +343,50 @@
 ):
     prompts = prefix_cache.shape[0]
     beams = prompts * BW
-    pages = tail_cache.reshape(beams, PAGE, 2 * HD)
     bias = qkv_bias.reshape(GROUP + 2, HD)
     table = rope_rows()
     swap = functools.partial(
         lax.all_to_all, axis_name="ctx", split_axis=0, concat_axis=0, tiled=True
     )
 
-    parts, moved, seen = call(
+    tail = BW * PAGE
+    load = SHARE + 2 * prefix_cache.shape[1] + 2 * tail
+    parts, seen, pick = call(
         project_kernel,
         [
-            ((prompts, SHARE, HD), BF16),
-            ((CTX, 2 * PAGE, HD), BF16),
-            ((prompts + 2, ROWS, HD), F32),
+            ((prompts, load, HD), BF16),
+            ((LX * LC + 2, ROWS, HD), F32),
+            ((tail, HD), BF16),
         ],
-        [SMEM] * 2 + [HBM] * 5,
+        [SMEM] * 2 + [HBM] * 6,
         [
             pltpu.VMEM(hidden.shape, BF16),
             pltpu.VMEM(qkv_weight.shape, BF16),
             pltpu.VMEM(bias.shape, BF16),
             pltpu.VMEM(table.shape, F32),
-            pltpu.VMEM(pages.shape, BF16),
-            pltpu.SemaphoreType.DMA((5,)),
+            pltpu.SemaphoreType.DMA((4 + 4 * prompts,)),
         ],
         limit=60,
-    )(parents, start_dev, hidden, qkv_weight, bias, table, pages)
-    parts = swap(parts, axis_index_groups=ALONG_XC)
-    (parts,) = call(row_sum_kernel, [((LY, SHARE, HD), BF16)], [VMEM])(parts)
+    )(
+        parents,
+        start_dev,
+        hidden,
+        qkv_weight,
+        bias,
+        table,
+        prefix_cache,
+        tail_cache.reshape(beams * PAGE, 2 * HD),
+    )
+    cache = swap(parts, axis_index_groups=ALONG_XC)
+    (parts,) = call(row_sum_kernel, [((LY, SHARE, HD), BF16)], [VMEM])(cache)
+    sums = swap(parts, axis_index_groups=ALONG_Y)
+    parts, own = call(
+        attend_kernel,
+        [((LY, PACK, HD), BF16), ((SHARE, HD), BF16)],
+        [VMEM] * 4,
+        [pltpu.VMEM((prompts, KEYS_AT, prefix_cache.shape[1] + tail), F32)],
+    )(sums, cache, seen, pick)
     parts = swap(parts, axis_index_groups=ALONG_Y)
-    mine, own = call(
-        sum_kernel, [((prompts, KEYS_AT, HD), BF16), ((SHARE, HD), BF16)], [VMEM]
-    )(parts)
-    shared = swap(mine, axis_index_groups=ALONG_XC)
-    (parts,) = call(attend_kernel, [((CTX, PACK, HD), BF16)], [VMEM] * 5)(
-        shared, prefix_cache, pages, seen, moved
-    )
-    parts = swap(parts)
     (merged,) = call(merge_kernel, [((CTX, CARRY, HD), BF16)], [VMEM] * 3)(parts, own, seen)
     heads = swap(merged)
     (share,) = call(output_kernel, [((prompts, ROWS, HD), BF16)], [VMEM] * 2)(heads, out_weight)

time: 129 us -> 123 us (0.953)
  blocking collectives: 120 us -> 114 us
    all_to_all x3 -> x2, blocking collectives: 58.9 us -> 50 us  [the longest x1 35 us: per_device(): cache = swap(parts, axis_index_groups=ALONG_XC)]
    all_to_all x1, blocking collectives: 14.9 us -> 18.9 us  [per_device(): parts = swap(parts, axis_index_groups=ALONG_Y)]
    pallas_call x4 -> x3, Pallas kernels: 5.68 us -> 5.05 us  [the longest x1 3.78 us: per_device(): call(project_kernel, [((prompts, load, HD), BF16), ((LX * LC + 2, ROWS, H...]
where the time goes in v4:
time: 123 us; the launch traced here: 122 us
  blocking collectives  114 us (93%)
  Pallas kernels  7.24 us (6%)
    all_to_all x1, blocking collectives, per_device(): cache = swap(parts, axis_index_groups=ALONG_XC)  35 us
    all_to_all x1, blocking collectives, per_device(): heads = swap(merged)  29.4 us
    all_to_all x1, blocking collectives, per_device(): parts = swap(parts, axis_index_groups=ALONG_Y)  18.9 us
    all_to_all x1, blocking collectives, per_device(): share = swap(share, axis_name='tp')  16 us
    all_to_all x1, blocking collectives, per_device(): sums = swap(parts, axis_index_groups=ALONG_Y)  15 us
    pallas_call x1, Pallas kernels, per_device(): call(project_kernel, [((prompts, load, HD), BF16), ((LX * LC + 2, ROWS, H...  3.78 us

profile of v4, /device:TPU:1, one launch (start us, length us, event | category | flops | bytes accessed | tf_op | source)
XLA Modules:
  0.0 122.3 jit_solution(967865524749131894)
XLA Ops:
  0.6 3.8 %shard_map.104 = (bf16[8,928,128]{2,1,0:T(8,128)(2,1)}, f32[10,16,128]{2,1,0:T(8,128)}, bf16[128,128]{1,0:T(8,128)(2,1)}) custom-call(s32[2,64]{1,0:T(2,128)} %parents_ref.1, s32[3,64]{1,0:T(4,128)} %start_ref.1, bf16[2,64,128]{2,1,0:T(8,128)(2,1)} %hidden_hbm.1, bf16[128,1280]{1,0:T(8,128)(2,1)} %weight_hbm.1, bf16[10,128]{1,0:T(8,128)(2,1)} %bitcast.8, ...), custom_call_target="tpu_custom_call" | custom-call | tf_op jit(solution)/shard_map/pallas_call | solution.py:354
  4.4 35.0 %all_to_all.25.parts_ref.cache_ref = bf16[8,928,128]{2,1,0:T(8,128)(2,1)S(1)} all-to-all(bf16[8,928,128]{2,1,0:T(8,128)(2,1)} %get-tuple-element.9), channel_id=1, replica_groups={{0,8,128,136,256,264,384,392},{16,24,144,152,272,280,400,408},{32,40,16..., dimensions={0} | all-to-all | bytes 3801088 | tf_op jit(solution)/shard_map/all_to_all | solution.py:380
  39.4 0.0 copy-start
  39.4 0.0 copy-start.2
  39.5 15.0 %all_to_all.26.sums_ref = bf16[8,160,128]{2,1,0:T(8,128)(2,1)S(1)} all-to-all(bf16[8,160,128]{2,1,0:T(8,128)(2,1)S(1)} %shard_map.105), channel_id=1, replica_groups={{0,16,32,48,64,80,96,112},{8,24,40,56,72,88,104,120},{128,144,160,176,1..., dimensions={0} | all-to-all | bytes 655360 | tf_op jit(solution)/shard_map/all_to_all | solution.py:382
  54.5 0.0 copy-done
  54.5 0.0 copy-done.2
  54.5 1.2 %shard_map.106 = (bf16[8,280,128]{2,1,0:T(8,128)(2,1)S(1)}, bf16[160,128]{1,0:T(8,128)(2,1)S(1)}) custom-call(bf16[8,160,128]{2,1,0:T(8,128)(2,1)S(1)} %all_to_all.26.sums_ref, bf16[8,928,128]{2,1,0:T(8,128)(2,1)S(1)} %all_to_all.25.parts_ref.cache_ref, f32[10,16,128]{2,1,0:T(8,128)S(1)} %copy-done, bf16[128,128]{1,0:T(8,128)(2,1)S(1)} %copy-done.2), custom_call_target="tpu_custom_call" | custom-call | tf_op jit(solution)/shard_map/pallas_call | solution.py:383
  55.7 0.0 copy-start.1
  55.7 18.9 %all_to_all.27.parts_ref = bf16[8,280,128]{2,1,0:T(8,128)(2,1)S(1)} all-to-all(bf16[8,280,128]{2,1,0:T(8,128)(2,1)S(1)} %get-tuple-element.12), channel_id=1, replica_groups={{0,16,32,48,64,80,96,112},{8,24,40,56,72,88,104,120},{128,144,160,176,1..., dimensions={0} | all-to-all | bytes 1146880 | tf_op jit(solution)/shard_map/all_to_all | solution.py:389
  74.7 0.6 shard_map.107
  75.3 29.4 %all_to_all.28.heads_ref = bf16[64,48,128]{2,1,0:T(8,128)(2,1)S(1)} all-to-all(bf16[64,48,128]{2,1,0:T(8,128)(2,1)S(1)} %shard_map.107), channel_id=1, replica_groups=mesh['ctx'=64,'tp'=8] {'ctx'}, dimensions={0} | all-to-all | bytes 1572864 | tf_op jit(solution)/shard_map/all_to_all | solution.py:391
  104.7 0.0 copy-done.1
  104.7 0.2 shard_map.108
  104.9 16.0 %all_to_all.29.share_ref = bf16[8,16,128]{2,1,0:T(8,128)(2,1)S(1)} all-to-all(bf16[8,16,128]{2,1,0:T(8,128)(2,1)S(1)} %shard_map.108), channel_id=1, replica_groups=mesh['ctx'=64,'tp'=8] {'tp'}, dimensions={0} | all-to-all | bytes 65536 | tf_op jit(solution)/shard_map/all_to_all | solution.py:393
  120.9 1.4 %shard_map.109 = (bf16[2,8,128]{2,1,0:T(8,128)(2,1)}, bf16[4,2,8,16,256]{4,3,2,1,0:T(8,128)(2,1)}) custom-call(bf16[8,16,128]{2,1,0:T(8,128)(2,1)S(1)} %all_to_all.29.share_ref, bf16[4,8,2,48,128]{4,3,2,1,0:T(8,128)(2,1)S(1)} %bitcast.6), custom_call_target="tpu_custom_call" | custom-call | tf_op jit(solution)/shard_map/pallas_call | solution.py:394
  (1 shorter events, 0.0 us)
Async XLA Ops:
  39.4 15.1 %copy-start = (f32[10,16,128]{2,1,0:T(8,128)S(1)}, f32[10,16,128]{2,1,0:T(8,128)}, u32[]{:S(2)}) copy-start(f32[10,16,128]{2,1,0:T(8,128)} %get-tuple-element.10.seen_ref) | copy-start | bytes 245764
  39.4 15.1 %copy-start.2 = (bf16[128,128]{1,0:T(8,128)(2,1)S(1)}, bf16[128,128]{1,0:T(8,128)(2,1)}, u32[]{:S(2)}) copy-start(bf16[128,128]{1,0:T(8,128)(2,1)} %get-tuple-element.11.pick_ref) | copy-start | bytes 98308
  55.7 48.9 %copy-start.1 = (bf16[1024,128]{1,0:T(8,128)(2,1)S(1)}, bf16[1024,128]{1,0:T(8,128)(2,1)}, u32[]{:S(2)}) copy-start(bf16[1024,128]{1,0:T(8,128)(2,1)} %weight_ref.1) | copy-start | bytes 786436
